TPU v7x, 32 devices: a whole 2x2x4 slice. The times are simulated.
32 devices in a mesh: resp: 4 (over y, core), dp: 8 (over z, x).
Axes of the slice: x: 2, y: 2, z: 4, core: 2. Of those that a mesh axis runs over, the one named last changes fastest.
Arguments:
- query_in: bfloat16 [4, 8, 128, 2560], P('resp', 'dp'), may hold values from -8 to 8
- key_in: bfloat16 [4, 8, 128, 512], P('resp', 'dp'), may hold values from -8 to 8
- value_in: bfloat16 [4, 8, 128, 512], P('resp', 'dp'), may hold values from -6 to 6
- prefix_key: bfloat16 [4, 8, 256, 512], P('resp', 'dp'), may hold values from -6 to 6
- prefix_value: bfloat16 [4, 8, 256, 512], P('resp', 'dp'), may hold values from -6 to 6
- q_bias: bfloat16 [2560], replicated, may hold values from -2 to 2
- out_grad: bfloat16 [4, 8, 128, 2560], P('resp', 'dp'), may hold values from -6 to 6
- group: int32 [4, 8], P('resp', 'dp'), may hold values from 0 to 3
- resp_len: int32 [4, 8], P('resp', 'dp'), may hold values from 1 to 128
- pref_blocks: int32 [4, 8], P('resp', 'dp'), may hold values from 1 to 2
- keep: int32 [4, 8, 2], P('resp', 'dp'), may hold values 0 or 1
Outputs:
- q_grad: bfloat16 [4, 8, 128, 2560], P('resp', 'dp')
- key_grad: bfloat16 [4, 8, 128, 512], P('resp', 'dp')
- value_grad: bfloat16 [4, 8, 128, 512], P('resp', 'dp')
- prefix_key_grad: bfloat16 [4, 8, 256, 512], P('resp', 'dp')
- prefix_value_grad: bfloat16 [4, 8, 256, 512], P('resp', 'dp')
- q_bias_grad: float32 [2560], replicated
- v_bias_grad: float32 [512], replicated
All inputs are finite; a program needn't handle non-finite values. No bound on the sum of `keep` on one device may be relied on, other than what follows from the above.
Results may differ from a plain program's by a relative error of at most 0.012.
The roundings to bfloat16 on the way count: a program that leaves them out, or rounds other values in their place, can miss the bound.
Values may be sent and summed in bfloat16 or wider, within the bound.
No kernel may reach another device: no remote copies, remote signals or barrier semaphores. Data moves between devices by JAX's collectives and lax.ppermute only.
A program may use at most 64 MiB of HBM per device.

v0:
```python
import functools

import jax
import jax.numpy as jnp
from jax import lax
from jax.experimental import pallas as pl
from jax.experimental.pallas import tpu as pltpu
from jax.sharding import PartitionSpec as P

HEAD_DIM = 128
BLOCK = 128
CORES = 2
LOG2E = 1.4426950408889634
masked_score = -1e30
score_scale = HEAD_DIM ** (-0.5)

GROUP, HELD, SELF, LENGTH = 0, 1, 2, 3

NT = (((1,), (1,)), ((), ()))
NN = (((1,), (0,)), ((), ()))
TN = (((0,), (0,)), ((), ()))


def dot(a, b, dims):
    return lax.dot_general(a, b, dims, preferred_element_type=jnp.float32)


def head(n):
    return pl.ds(n * HEAD_DIM, HEAD_DIM)


def heads(k, gsize):
    return pl.ds(k * gsize * HEAD_DIM, gsize * HEAD_DIM)


def info_kernel(me_ref, group_ref, held_ref, len_ref, info_ref):
    def note(row, value):
        info_ref[row : row + 1, :] = jnp.broadcast_to(value, (1, HEAD_DIM))

    note(GROUP, group_ref[...])
    note(HELD, held_ref[...])
    note(SELF, me_ref[...])
    note(LENGTH, len_ref[...])


def self_kernel(
    kv_heads,
    gsize,
    info_ref,
    bias_hbm,
    k_hbm,
    v_hbm,
    q_hbm,
    og_hbm,
    qs_ref,
    gs_ref,
    ss_ref,
    dp_ref,
    bias_ref,
    k_ref,
    v_ref,
    q_ref,
    og_ref,
    sems,
):
    rows = q_ref.shape[0]
    copies = []

    def fetch(src, dst):
        copies.append(pltpu.make_async_copy(src, dst, sems.at[len(copies)]))
        copies[-1].start()

    for k in range(kv_heads):
        cols = heads(k, gsize)
        if not k:
            fetch(bias_hbm, bias_ref)
            fetch(k_hbm, k_ref)
        fetch(q_hbm.at[:, cols], q_ref.at[:, cols])
        if not k:
            fetch(v_hbm, v_ref)
        fetch(og_hbm.at[:, cols], og_ref.at[:, cols])

    pos_u = lax.broadcasted_iota(jnp.int32, (rows, rows), 0)
    pos_t = lax.broadcasted_iota(jnp.int32, (rows, rows), 1)
    causal = pos_u <= pos_t
    live = lax.broadcasted_iota(jnp.int32, (rows, HEAD_DIM), 0) < info_ref[LENGTH : LENGTH + 1, :]
    copies[0].wait()
    bias = bias_ref[...].astype(jnp.float32)
    for k in range(kv_heads):
        for copy in copies[1:5] if not k else copies[3 + 2 * k : 5 + 2 * k]:
            copy.wait()
        keys = k_ref[:, head(k)]
        vals = v_ref[:, head(k)]
        for g in range(gsize):
            n = k * gsize + g
            q = (q_ref[:, head(n)].astype(jnp.float32) + bias[n : n + 1, :]).astype(jnp.bfloat16)
            qs_ref[k, head(g), :] = q
            grad = jnp.where(live, og_ref[:, head(n)].astype(jnp.float32), 0.0).astype(jnp.bfloat16)
            gs_ref[k, head(g), :] = grad
            ss_ref[k, :, head(g)] = jnp.where(causal, dot(keys, q, NT), masked_score)
            dp_ref[k, :, head(g)] = dot(vals, grad, NT)


def one_if(hit, dtype):
    return jnp.where(hit, 1.0, 0.0).astype(dtype)


def source_masks(infos, dtype):
    group = infos[0][GROUP : GROUP + 1, :]
    return [one_if(info[SELF : SELF + 1, :] == group, dtype) for info in infos]


def pick(refs, masks, k, b=0, size=None):
    total = None
    for ref, mask in zip(refs, masks):
        rows = slice(None)
        if isinstance(ref, tuple):
            ref = ref[b]
        elif size is not None:
            rows = pl.ds(b * size, size)
        term = ref[rows, head(k)] * mask
        total = term if total is None else total + term
    return total


def prob_kernel(kv_heads, gsize, count, whole, *refs):
    infos, refs = refs[:count], refs[count:]
    ka_ref, pa_ref, dvp_ref, dvs_ref, vb_ref, s_ref = refs[-6:]
    keep_ref, qs_ref, gs_ref, ss_ref, k_ref = refs[-11:-6]
    far_refs = refs[whole:-11]
    rows = k_ref.shape[0]
    prefix_len = ka_ref.shape[0] - rows
    blocks = prefix_len // BLOCK
    key_refs = list(refs[:whole]) + [far_refs[i : i + blocks] for i in range(0, len(far_refs), blocks)]
    masks = source_masks(infos, jnp.bfloat16)
    group = infos[0][GROUP : GROUP + 1, :]
    held = jnp.zeros_like(group)
    for info in infos:
        held = held + jnp.where(info[SELF : SELF + 1, :] == group, info[HELD : HELD + 1, :], 0)
    allow = []
    for b in range(blocks):
        keep = jnp.broadcast_to(keep_ref[:, b : b + 1], (1, HEAD_DIM))
        allow.append(jnp.where((held > b) & (keep == 1), 0.0, masked_score))
    scale = score_scale * LOG2E

    def scores(k):
        for b in range(blocks):
            ka_ref[pl.ds(b * BLOCK, BLOCK), head(k)] = pick(key_refs, masks, k, b, BLOCK)
        ka_ref[pl.ds(prefix_len, rows), head(k)] = k_ref[:, head(k)]
        s_ref[k % 2] = dot(ka_ref[pl.ds(0, prefix_len), head(k)], qs_ref[k], NT)

    def values(k):
        dval = dot(pa_ref[k], gs_ref[k], NN)
        dvp_ref[:, head(k)] = dval[:prefix_len].astype(jnp.bfloat16)
        dvs_ref[:, head(k)] = dval[prefix_len:].astype(jnp.bfloat16)
        vb_ref[k : k + 1, :] = jnp.sum(dval, axis=0, keepdims=True)

    scores(0)
    for k in range(kv_heads):
        if k + 1 < kv_heads:
            scores(k + 1)
        for g in range(gsize):
            own = ss_ref[k, :, head(g)]
            parts = [s_ref[k % 2, pl.ds(b * BLOCK, BLOCK), head(g)] for b in range(blocks)]
            peak = jnp.max(own, axis=0, keepdims=True)
            for b in range(blocks):
                peak = jnp.maximum(peak, jnp.max(parts[b], axis=0, keepdims=True) + allow[b])
            peak = peak * scale
            parts = [jnp.exp2(parts[b] * scale - (peak - allow[b])) for b in range(blocks)]
            parts.append(jnp.exp2(own * scale - peak))
            total = sum(jnp.sum(e, axis=0, keepdims=True) for e in parts)
            inverse = 1.0 / total
            for b in range(blocks + 1):
                pa_ref[k, pl.ds(b * BLOCK, BLOCK), head(g)] = (parts[b] * inverse).astype(jnp.bfloat16)
        if k:
            values(k - 1)
    values(kv_heads - 1)


def score_kernel(kv_heads, gsize, count, *refs):
    infos, refs = refs[:count], refs[count:]
    ds_ref, share_ref, vp_ref, d_ref = refs[-4:]
    gs_ref, pa_ref, dp_ref, ka_ref, vb_ref = refs[-9:-4]
    val_refs = refs[:-9]
    prefix_len = vp_ref.shape[1]
    blocks = prefix_len // BLOCK
    masks = source_masks(infos, jnp.bfloat16)
    cols = gsize * HEAD_DIM
    ones = (
        lax.broadcasted_iota(jnp.int32, (16, cols), 0) == lax.broadcasted_iota(jnp.int32, (16, cols), 1) // HEAD_DIM
    ).astype(jnp.bfloat16)

    def products(k):
        for b in range(blocks):
            vp_ref[k % 2, pl.ds(b * BLOCK, BLOCK), :] = pick(val_refs, masks, k, b, BLOCK)
        d_ref[k % 2] = dot(vp_ref[k % 2], gs_ref[k], NT)

    def finish(k):
        sums = dot(ones, ds_ref[k], NT)
        high = sums.astype(jnp.bfloat16)
        low = (sums - high.astype(jnp.float32)).astype(jnp.bfloat16)
        keys = ka_ref[:, head(k)]
        share = dot(high, keys, NN) + dot(low, keys, NN)
        share_ref[k * gsize : (k + 1) * gsize, :] = share[:gsize, :] * score_scale

    products(0)
    for k in range(kv_heads):
        if k + 1 < kv_heads:
            products(k + 1)
        for g in range(gsize):
            probs = [pa_ref[k, pl.ds(b * BLOCK, BLOCK), head(g)].astype(jnp.float32) for b in range(blocks + 1)]
            grads = [d_ref[k % 2, pl.ds(b * BLOCK, BLOCK), head(g)] for b in range(blocks)]
            grads.append(dp_ref[k, :, head(g)])
            delta = sum(jnp.sum(p * d, axis=0, keepdims=True) for p, d in zip(probs, grads))
            for b in range(blocks + 1):
                ds_ref[k, pl.ds(b * BLOCK, BLOCK), head(g)] = (probs[b] * (grads[b] - delta)).astype(jnp.bfloat16)
        if k:
            finish(k - 1)
    finish(kv_heads - 1)
    share_ref[kv_heads * gsize : kv_heads * (gsize + 1), :] = vb_ref[...]


def key_kernel(kv_heads, ds_ref, qs_ref, dkp_ref):
    prefix_len = dkp_ref.shape[0]
    for k in range(kv_heads):
        dkey = dot(ds_ref[k, pl.ds(0, prefix_len), :], qs_ref[k], NN)
        dkp_ref[:, head(k)] = (dkey * score_scale).astype(jnp.bfloat16)


def grad_kernel(kv_heads, gsize, ds_ref, ka_ref, qs_ref, qg_ref, kg_ref):
    rows = kg_ref.shape[0]
    prefix_len = ka_ref.shape[0] - rows
    for k in range(kv_heads):
        keys = ka_ref[:, head(k)]
        dkey = dot(ds_ref[k, pl.ds(prefix_len, rows), :], qs_ref[k], NN)
        kg_ref[:, head(k)] = (dkey * score_scale).astype(jnp.bfloat16)
        for g in range(gsize):
            dq = dot(ds_ref[k, :, head(g)], keys, TN)
            qg_ref[:, head(k * gsize + g)] = (dq * score_scale).astype(jnp.bfloat16)


def sum_kernel(count, *refs):
    infos, pieces, out_ref = refs[:count], refs[count : 2 * count], refs[2 * count]
    me = infos[0][SELF : SELF + 1, :]
    masks = [one_if(info[GROUP : GROUP + 1, :] == me, jnp.float32) for info in infos]
    for k in range(out_ref.shape[1] // HEAD_DIM):
        total = pieces[0][:, head(k)].astype(jnp.float32) * masks[0]
        for piece, mask in zip(pieces[1:], masks[1:]):
            total = total + piece[:, head(k)].astype(jnp.float32) * mask
        out_ref[:, head(k)] = total.astype(jnp.bfloat16)


def last_kernel(devices, *refs):
    shares, (qb_ref, vb_ref) = refs[:-2], refs[-2:]
    total = tree_sum([share[...] for share in shares]) / devices
    width = qb_ref.shape[0]
    qb_ref[...] = total[:width, :]
    vb_ref[...] = total[width:, :]


def tree_sum(terms):
    while len(terms) > 1:
        terms = [a + b for a, b in zip(terms[::2], terms[1::2])]
    return terms[0]


VMEM = pl.BlockSpec(memory_space=pltpu.VMEM)
SMEM = pl.BlockSpec(memory_space=pltpu.SMEM)
HBM = pl.BlockSpec(memory_space=pltpu.HBM)


def call(body, outs, in_specs, size=1000, scratch=()):
    return pl.pallas_call(
        body,
        out_shape=outs,
        in_specs=in_specs,
        out_specs=[VMEM] * len(outs),
        scratch_shapes=list(scratch),
        cost_estimate=pl.CostEstimate(flops=1000, bytes_accessed=size, transcendentals=0),
        compiler_params=pltpu.CompilerParams(vmem_limit_bytes=32 << 20),
    )


def in_hbm(x):
    return pltpu.with_memory_space_constraint(x, pltpu.HBM)


def after(xs, done):
    return lax.optimization_barrier((xs, done))[0]


def shifted(x, axis, count, cores, step, flip):
    pairs = []
    for i in range(count):
        chip, core = i // cores, i % cores
        to = ((chip + step) % (count // cores)) * cores + (core ^ flip)
        pairs.append((i, to))
    return lax.ppermute(x, axis, pairs)


def step_terms(x, bits, count):
    flips = [0]
    for bit in bits:
        flips += [flip ^ bit for flip in flips]
    return [x] + [lax.ppermute(x, ("resp", "dp"), [(i, i ^ flip) for i in range(count)]) for flip in flips[1:]]


def step_sum(x, bits, count, beside):
    return tree_sum(after(step_terms(x, bits, count), beside))


def per_device(
    holders,
    batches,
    query_in,
    key_in,
    value_in,
    prefix_key,
    prefix_value,
    q_bias,
    out_grad,
    group,
    resp_len,
    pref_blocks,
    keep,
):
    rows, width_q = query_in.shape[2:]
    prefix_len, width_kv = prefix_key.shape[2:]
    kv_heads = width_kv // HEAD_DIM
    gsize = width_q // width_kv
    cores = CORES if holders % CORES == 0 else 1
    chips = holders // cores
    bf, f32 = jnp.bfloat16, jnp.float32
    shape = jax.ShapeDtypeStruct

    def across(x):
        return [shifted(x, "resp", holders, cores, step, 0) for step in range(1, chips)]

    def to_core(xs):
        return [shifted(x, "resp", holders, cores, 0, 1) for x in xs] if cores > 1 else []

    def in_blocks(xs):
        return [x[b : b + BLOCK] for x in xs for b in range(0, prefix_len, BLOCK)]

    def summed(*pieces):
        (total,) = call(
            functools.partial(sum_kernel, count), [shape((prefix_len, width_kv), bf)], [VMEM] * (2 * count)
        )(*infos, *pieces)
        return total

    def spread(x):
        near = [x] + across(x)
        return near + to_core(near)

    own_keys, own_vals = prefix_key[0, 0], prefix_value[0, 0]
    vals_across = across(own_vals)
    keys_across = across(own_keys)
    keys_core = to_core([own_keys])
    vals_core = to_core([own_vals])
    count = holders

    me = lax.axis_index("resp").astype(jnp.int32).reshape(1, 1)
    (info,) = call(info_kernel, [shape((8, HEAD_DIM), jnp.int32)], [VMEM] * 4)(
        me, group, pref_blocks, resp_len
    )
    queries, grads, s_self, d_self = call(
        functools.partial(self_kernel, kv_heads, gsize),
        [
            shape((kv_heads, gsize * rows, HEAD_DIM), bf),
            shape((kv_heads, gsize * rows, HEAD_DIM), bf),
            shape((kv_heads, rows, gsize * rows), f32),
            shape((kv_heads, rows, gsize * rows), f32),
        ],
        [VMEM] + [HBM] * 5,
        scratch=[
            pltpu.VMEM((kv_heads * gsize, HEAD_DIM), bf),
            pltpu.VMEM((rows, width_kv), bf),
            pltpu.VMEM((rows, width_kv), bf),
            pltpu.VMEM((rows, width_q), bf),
            pltpu.VMEM((rows, width_q), bf),
            pltpu.SemaphoreType.DMA((3 + 2 * kv_heads,)),
        ],
    )(
        info,
        *map(
            in_hbm,
            (q_bias.reshape(-1, HEAD_DIM), key_in[0, 0], value_in[0, 0], query_in[0, 0], out_grad[0, 0]),
        ),
    )
    infos = spread(info)
    keys_across = after(keys_across, (infos[: chips + 1], d_self))
    keys_core = after(keys_core, keys_across)
    keys_across = after(keys_across, keys_core)
    keys_far = to_core(in_blocks(keys_across))
    keys_near = [own_keys, *keys_across, *keys_core]

    all_keys, probs, dval_pre, dval_self, v_share = call(
        functools.partial(prob_kernel, kv_heads, gsize, count, len(keys_near)),
        [
            shape((prefix_len + rows, width_kv), bf),
            shape((kv_heads, prefix_len + rows, gsize * rows), bf),
            shape((prefix_len, width_kv), bf),
            shape((rows, width_kv), bf),
            shape((kv_heads, HEAD_DIM), f32),
        ],
        [VMEM] * (count + len(keys_near) + len(keys_far) + 5),
        scratch=[pltpu.VMEM((2, prefix_len, gsize * rows), f32)],
    )(*infos, *keys_near, *keys_far, keep[0], queries, grads, s_self, key_in[0, 0])
    dvals_across = across(dval_pre)
    vals_across = after(vals_across, v_share)
    vals_moved = [own_vals, *vals_across, *vals_core, *to_core(vals_across)]

    dscores, share = call(
        functools.partial(score_kernel, kv_heads, gsize, count),
        [
            shape((kv_heads, prefix_len + rows, gsize * rows), bf),
            shape((kv_heads * (gsize + 1), HEAD_DIM), f32),
        ],
        [VMEM] * (2 * count + 5),
        scratch=[
            pltpu.VMEM((2, prefix_len, HEAD_DIM), bf),
            pltpu.VMEM((2, prefix_len, gsize * rows), f32),
        ],
    )(*infos, *vals_moved, grads, probs, d_self, all_keys, v_share)
    (dkey_pre,) = call(
        functools.partial(key_kernel, kv_heads), [shape((prefix_len, width_kv), bf)], [VMEM] * 2
    )(dscores, queries)
    dvals_core = to_core([after(dval_pre, dkey_pre)])
    dkeys_across = across(dkey_pre)
    dkeys_core = to_core([dkey_pre])

    devices = holders * batches
    bits = [1 << i for i in range(devices.bit_length() - 1)]
    dp_bits = [bit for bit in bits if bit < batches]
    core_bits = [bit for bit in bits if batches <= bit < batches * cores]
    y_bits = [bit for bit in bits if bit >= batches * cores]
    share = step_sum(share, dp_bits[:1], devices, dkey_pre)

    q_grad, key_grad = call(
        functools.partial(grad_kernel, kv_heads, gsize),
        [shape((rows, width_q), bf), shape((rows, width_kv), bf)],
        [VMEM] * 3,
    )(after(dscores, share), all_keys, queries)

    for i in range(1, len(dp_bits), 2):
        share = step_sum(share, dp_bits[i : i + 2], devices, key_grad)
    dvals_across = after(dvals_across, share)
    prefix_value_grad = summed(dval_pre, *dvals_across, *dvals_core, *to_core(dvals_across))
    dkeys_across = after(dkeys_across, (share, key_grad))
    prefix_key_grad = summed(dkey_pre, *dkeys_across, *dkeys_core, *to_core(dkeys_across))

    for bit in y_bits[1:]:
        share = step_sum(share, [bit], devices, prefix_value_grad)
    shares = after(step_terms(share, core_bits + y_bits[:1], devices), (prefix_value_grad, prefix_key_grad))
    q_total, v_total = call(
        functools.partial(last_kernel, devices),
        [shape((kv_heads * gsize, HEAD_DIM), f32), shape((kv_heads, HEAD_DIM), f32)],
        [VMEM] * len(shares),
    )(*shares)

    return (
        q_grad[None, None],
        key_grad[None, None],
        dval_self[None, None],
        prefix_key_grad[None, None],
        prefix_value_grad[None, None],
        q_total.reshape(width_q),
        v_total.reshape(width_kv),
    )


def solution(mesh):
    holders, batches = mesh.shape["resp"], mesh.shape["dp"]
    wide = P("resp", "dp", None, None)
    ints = P("resp", "dp")
    in_specs = (wide,) * 5 + (P(), wide, ints, ints, ints, P("resp", "dp", None))
    out_specs = (wide,) * 5 + (P(), P())
    return jax.shard_map(
        functools.partial(per_device, holders, batches),
        mesh=mesh,
        in_specs=in_specs,
        out_specs=out_specs,
        check_vma=False,
    )
```

profile of v0, /device:TPU:0, one launch (start us, length us, event | category | flops | bytes accessed | tf_op | source)
XLA Modules:
  0.0 38.3 jit_solution(11125374204736831792)
XLA Ops:
  0.6 0.0 copy-start.2
  0.7 0.0 copy-start
  0.7 3.0 %collective-permute-start.4 = (bf16[256,512]{1,0:T(8,128)(2,1)}, bf16[256,512]{1,0:T(8,128)(2,1)S(1)}, u32[]{:S(2)}, u32[]{:S(2)}) collective-permute-start(bf16[256,512]{1,0:T(8,128)(2,1)} %bitcast.18), channel_id=1, source_target_pairs={{0,16},{8,24},{16,0},{24,8},{1,17},{9,25},{17,1},{25,9},{2,18},{10... | collective-permute-start | bytes 786440 | tf_op jit(solution)/shard_map/ppermute | solution.py:298
  3.7 0.0 collective-permute-start.5
  5.7 0.1 shard_map.162.info_ref.refs_0_
  5.7 0.5 %collective-permute-start.1 = (s32[8,128]{1,0:T(8,128)S(1)}, s32[8,128]{1,0:T(8,128)S(1)}, u32[]{:S(2)}, u32[]{:S(2)}) collective-permute-start(s32[8,128]{1,0:T(8,128)S(1)} %shard_map.162.info_ref.refs_0_), channel_id=1, source_target_pairs={{0,8},{8,0},{16,24},{24,16},{1,9},{9,1},{17,25},{25,17},{2,10},{10... | collective-permute-start | bytes 12296 | tf_op jit(solution)/shard_map/ppermute | solution.py:298
  6.2 0.1 collective-permute-start
  6.3 1.9 %collective-permute-start.3 = (bf16[256,512]{1,0:T(8,128)(2,1)}, bf16[256,512]{1,0:T(8,128)(2,1)S(1)}, u32[]{:S(2)}, u32[]{:S(2)}) collective-permute-start(bf16[256,512]{1,0:T(8,128)(2,1)} %bitcast.21), channel_id=1, source_target_pairs={{0,16},{8,24},{16,0},{24,8},{1,17},{9,25},{17,1},{25,9},{2,18},{10... | collective-permute-start | bytes 786440 | tf_op jit(solution)/shard_map/ppermute | solution.py:298
  8.3 2.7 %shard_map.163 = (bf16[4,640,128]{2,1,0:T(8,128)(2,1)S(1)}, bf16[4,640,128]{2,1,0:T(8,128)(2,1)S(1)}, f32[4,128,640]{2,1,0:T(8,128)S(1)}, f32[4,128,640]{2,1,0:T(8,128)S(1)}) custom-call(s32[8,128]{1,0:T(8,128)S(1)} %shard_map.162.info_ref.refs_0_, bf16[20,128]{1,0:T(8,128)(2,1)} %bitcast.30, bf16[128,512]{1,0:T(8,128)(2,1)} %bitcast.16, ...), custom_call_target="tpu_custom_call" | custom-call | flops 1000 | bytes 1000 | tf_op jit(solution)/shard_map/pallas_call | solution.py:366
  10.9 0.0 collective-permute-done.1.refs_2_
  11.0 0.2 collective-permute-done.refs_1_
  11.1 0.0 collective-permute-done.4.refs_5_
  11.1 0.0 collective-permute-done.5.refs_6_
  11.2 0.1 collective-permute-start.7
  11.3 0.5 %collective-permute-start.6 = (bf16[128,512]{1,0:T(8,128)(2,1)S(1)}, bf16[128,512]{1,0:T(8,128)(2,1)S(1)}, u32[]{:S(2)}, u32[]{:S(2)}) collective-permute-start(bf16[128,512]{1,0:T(8,128)(2,1)S(1)} %get-tuple-element.74), channel_id=1, source_target_pairs={{0,8},{8,0},{16,24},{24,16},{1,9},{9,1},{17,25},{25,17},{2,10},{10... | collective-permute-start | bytes 393224 | tf_op jit(solution)/shard_map/ppermute | solution.py:298
  11.7 0.1 collective-permute-start.2
  11.8 0.4 %collective-permute-start.8 = (bf16[256,512]{1,0:T(8,128)(2,1)S(1)}, bf16[256,512]{1,0:T(8,128)(2,1)S(1)}, u32[]{:S(2)}, u32[]{:S(2)}) collective-permute-start(bf16[256,512]{1,0:T(8,128)(2,1)S(1)} %bitcast.22), channel_id=1, source_target_pairs={{0,8},{8,0},{16,24},{24,16},{1,9},{9,1},{17,25},{25,17},{2,10},{10... | collective-permute-start | bytes 786440 | tf_op jit(solution)/shard_map/ppermute | solution.py:298
  12.3 0.7 %collective-permute-done.2.refs_3_ = s32[8,128]{1,0:T(8,128)S(1)} collective-permute-done((s32[8,128]{1,0:T(8,128)S(1)}, s32[8,128]{1,0:T(8,128)S(1)}, u32[]{:S(2)}, u32[]{:S(2)}) %collective-permute-start.2) | collective-permute-done | bytes 4128 | tf_op jit(solution)/shard_map/ppermute | solution.py:298
  12.9 0.0 collective-permute-done.7.refs_8_
  12.9 0.0 collective-permute-done.6.refs_7_
  12.9 2.6 %shard_map.164 = (bf16[384,512]{1,0:T(8,128)(2,1)S(1)}, bf16[4,384,640]{2,1,0:T(8,128)(2,1)S(1)}, bf16[256,512]{1,0:T(8,128)(2,1)S(1)}, bf16[128,512]{1,0:T(8,128)(2,1)}, f32[4,128]{1,0:T(4,128)S(1)}) custom-call(s32[8,128]{1,0:T(8,128)S(1)} %shard_map.162.info_ref.refs_0_, s32[8,128]{1,0:T(8,128)S(1)} %collective-permute-done.refs_1_, ...), custom_call_target="tpu_custom_call" | custom-call | flops 1000 | bytes 1000 | tf_op jit(solution)/shard_map/pallas_call | solution.py:397
  15.5 0.4 %collective-permute-done.3.refs_5_ = bf16[256,512]{1,0:T(8,128)(2,1)S(1)} collective-permute-done((bf16[256,512]{1,0:T(8,128)(2,1)}, bf16[256,512]{1,0:T(8,128)(2,1)S(1)}, u32[]{:S(2)}, u32[]{:S(2)}) %collective-permute-start.3) | collective-permute-done | bytes 262176 | tf_op jit(solution)/shard_map/ppermute | solution.py:298
  15.9 1.8 %collective-permute-start.17 = (bf16[256,512]{1,0:T(8,128)(2,1)S(1)}, bf16[256,512]{1,0:T(8,128)(2,1)S(1)}, u32[]{:S(2)}, u32[]{:S(2)}) collective-permute-start(bf16[256,512]{1,0:T(8,128)(2,1)S(1)} %get-tuple-element.66.refs_4_), channel_id=1, source_target_pairs={{0,16},{8,24},{16,0},{24,8},{1,17},{9,25},{17,1},{25,9},{2,18},{10... | collective-permute-start | bytes 786440 | tf_op jit(solution)/shard_map/ppermute | solution.py:298
  17.8 0.0 collective-permute-done.9.refs_7_
  17.8 2.2 %shard_map.165 = (bf16[4,384,640]{2,1,0:T(8,128)(2,1)S(1)}, f32[24,128]{1,0:T(8,128)S(1)}) custom-call(s32[8,128]{1,0:T(8,128)S(1)} %shard_map.162.info_ref.refs_0_, s32[8,128]{1,0:T(8,128)S(1)} %collective-permute-done.refs_1_, s32[8,128]{1,0:T(8,128)S(1)} %collective-permute-done.1.refs_2_, s32[8,128]{1,0:T(8,128)S(1)} %collective-permute-done.2.refs_3_, ...), custom_call_target="tpu_custom_call" | custom-call | flops 1000 | bytes 1000 | tf_op jit(solution)/shard_map/pallas_call | solution.py:413
  19.9 1.5 %collective-permute-start.10 = (f32[24,128]{1,0:T(8,128)S(1)}, f32[24,128]{1,0:T(8,128)S(1)}, u32[]{:S(2)}, u32[]{:S(2)}) collective-permute-start(f32[24,128]{1,0:T(8,128)S(1)} %get-tuple-element.53), channel_id=1, source_target_pairs={{0,1},{1,0},{2,3},{3,2},{4,5},{5,4},{6,7},{7,6},{8,9},{9,8},{10,11... | collective-permute-start | bytes 36872 | tf_op jit(solution)/shard_map/ppermute | solution.py:305
  21.5 0.5 %shard_map.166.refs_4_ = bf16[256,512]{1,0:T(8,128)(2,1)S(1)} custom-call(bf16[4,384,640]{2,1,0:T(8,128)(2,1)S(1)} %get-tuple-element.55.ds_ref, bf16[4,640,128]{2,1,0:T(8,128)(2,1)S(1)} %get-tuple-element.44.refs_10_.qs_ref), custom_call_target="tpu_custom_call" | custom-call | flops 1000 | bytes 1000 | tf_op jit(solution)/shard_map/pallas_call | solution.py:425
  22.0 1.5 %collective-permute-start.11 = (bf16[256,512]{1,0:T(8,128)(2,1)S(1)}, bf16[256,512]{1,0:T(8,128)(2,1)S(1)}, u32[]{:S(2)}, u32[]{:S(2)}) collective-permute-start(bf16[256,512]{1,0:T(8,128)(2,1)S(1)} %shard_map.166.refs_4_), channel_id=1, source_target_pairs={{0,16},{8,24},{16,0},{24,8},{1,17},{9,25},{17,1},{25,9},{2,18},{10... | collective-permute-start | bytes 786440 | tf_op jit(solution)/shard_map/ppermute | solution.py:298
  23.5 0.2 collective-permute-done.10
  23.7 3.6 %collective-permute-start.14 = (f32[24,128]{1,0:T(8,128)S(1)}, f32[24,128]{1,0:T(8,128)S(1)}, u32[]{:S(2)}, u32[]{:S(2)}) collective-permute-start(f32[24,128]{1,0:T(8,128)S(1)} %add.12), channel_id=1, source_target_pairs={{0,6},{1,7},{2,4},{3,5},{4,2},{5,3},{6,0},{7,1},{8,14},{9,15},{10,... | collective-permute-start | bytes 36872 | tf_op jit(solution)/shard_map/ppermute | solution.py:305
  27.3 0.0 collective-permute-start.13
  27.3 0.8 %collective-permute-start.12 = (f32[24,128]{1,0:T(8,128)S(1)}, f32[24,128]{1,0:T(8,128)S(1)}, u32[]{:S(2)}, u32[]{:S(2)}) collective-permute-start(f32[24,128]{1,0:T(8,128)S(1)} %add.12), channel_id=1, source_target_pairs={{0,2},{1,3},{2,0},{3,1},{4,6},{5,7},{6,4},{7,5},{8,10},{9,11},{10,... | collective-permute-start | bytes 36872 | tf_op jit(solution)/shard_map/ppermute | solution.py:305
  28.0 1.7 %shard_map.167 = (bf16[128,2560]{1,0:T(8,128)(2,1)}, bf16[128,512]{1,0:T(8,128)(2,1)}) custom-call(bf16[4,384,640]{2,1,0:T(8,128)(2,1)S(1)} %get-tuple-element.55.ds_ref, bf16[384,512]{1,0:T(8,128)(2,1)S(1)} %get-tuple-element.50.refs_11_.ka_ref, bf16[4,640,128]{2,1,0:T(8,128)(2,1)S(1)} %get-tuple-element.44.refs_10_.qs_ref), custom_call_target="tpu_custom_call" | custom-call | flops 1000 | bytes 1000 | tf_op jit(solution)/shard_map/pallas_call | solution.py:439
  29.8 0.0 collective-permute-start.18
  29.8 2.1 %collective-permute-done.13 = f32[24,128]{1,0:T(8,128)S(1)} collective-permute-done((f32[24,128]{1,0:T(8,128)S(1)}, f32[24,128]{1,0:T(8,128)S(1)}, u32[]{:S(2)}, u32[]{:S(2)}) %collective-permute-start.13) | collective-permute-done | bytes 12320 | tf_op jit(solution)/shard_map/ppermute | solution.py:305
  31.9 0.0 collective-permute-done.17.refs_5_
  31.9 0.1 collective-permute-start.19
  32.0 0.5 %collective-permute-start.15 = (bf16[256,512]{1,0:T(8,128)(2,1)S(1)}, bf16[256,512]{1,0:T(8,128)(2,1)S(1)}, u32[]{:S(2)}, u32[]{:S(2)}) collective-permute-start(bf16[256,512]{1,0:T(8,128)(2,1)S(1)} %shard_map.166.refs_4_), channel_id=1, source_target_pairs={{0,8},{8,0},{16,24},{24,16},{1,9},{9,1},{17,25},{25,17},{2,10},{10... | collective-permute-start | bytes 786440 | tf_op jit(solution)/shard_map/ppermute | solution.py:298
  32.5 0.1 collective-permute-start.16
  32.5 1.5 %collective-permute-start.22 = (f32[24,128]{1,0:T(8,128)S(1)}, f32[24,128]{1,0:T(8,128)S(1)}, u32[]{:S(2)}, u32[]{:S(2)}) collective-permute-start(f32[24,128]{1,0:T(8,128)S(1)} %add_add_fusion.refs_0_), channel_id=1, source_target_pairs={{0,24},{1,25},{2,26},{3,27},{4,28},{5,29},{6,30},{7,31},{8,16},{9,... | collective-permute-start | bytes 36872 | tf_op jit(solution)/shard_map/ppermute | solution.py:305
  34.0 0.0 collective-permute-done.18.refs_6_
  34.0 0.6 %collective-permute-start.21 = (f32[24,128]{1,0:T(8,128)S(1)}, f32[24,128]{1,0:T(8,128)S(1)}, u32[]{:S(2)}, u32[]{:S(2)}) collective-permute-start(f32[24,128]{1,0:T(8,128)S(1)} %add_add_fusion.refs_0_), channel_id=1, source_target_pairs={{0,16},{1,17},{2,18},{3,19},{4,20},{5,21},{6,22},{7,23},{8,24},{9,... | collective-permute-start | bytes 36872 | tf_op jit(solution)/shard_map/ppermute | solution.py:305
  34.6 0.9 %shard_map.169 = bf16[256,512]{1,0:T(8,128)(2,1)} custom-call(s32[8,128]{1,0:T(8,128)S(1)} %shard_map.162.info_ref.refs_0_, s32[8,128]{1,0:T(8,128)S(1)} %collective-permute-done.refs_1_, s32[8,128]{1,0:T(8,128)S(1)} %collective-permute-done.1.refs_2_, s32[8,128]{1,0:T(8,128)S(1)} %collective-permute-done.2.refs_3_, ...), custom_call_target="tpu_custom_call" | custom-call | flops 1000 | bytes 1000 | tf_op jit(solution)/shard_map/pallas_call | solution.py:346
  35.5 0.0 collective-permute-done.15.refs_6_
  35.5 0.0 collective-permute-done.16.refs_7_
  35.5 0.9 %shard_map.168 = bf16[256,512]{1,0:T(8,128)(2,1)} custom-call(s32[8,128]{1,0:T(8,128)S(1)} %shard_map.162.info_ref.refs_0_, s32[8,128]{1,0:T(8,128)S(1)} %collective-permute-done.refs_1_, s32[8,128]{1,0:T(8,128)S(1)} %collective-permute-done.1.refs_2_, s32[8,128]{1,0:T(8,128)S(1)} %collective-permute-done.2.refs_3_, ...), custom_call_target="tpu_custom_call" | custom-call | flops 1000 | bytes 1000 | tf_op jit(solution)/shard_map/pallas_call | solution.py:346
  36.5 1.3 %collective-permute-done.21.refs_2_ = f32[24,128]{1,0:T(8,128)S(1)} collective-permute-done((f32[24,128]{1,0:T(8,128)S(1)}, f32[24,128]{1,0:T(8,128)S(1)}, u32[]{:S(2)}, u32[]{:S(2)}) %collective-permute-start.21) | collective-permute-done | bytes 12320 | tf_op jit(solution)/shard_map/ppermute | solution.py:305
  37.7 0.6 %shard_map.170 = (f32[20,128]{1,0:T(8,128)}, f32[4,128]{1,0:T(4,128)}) custom-call(f32[24,128]{1,0:T(8,128)S(1)} %add_add_fusion.refs_0_, f32[24,128]{1,0:T(8,128)S(1)} %collective-permute-done.20.refs_1_, f32[24,128]{1,0:T(8,128)S(1)} %collective-permute-done.21.refs_2_, f32[24,128]{1,0:T(8,128)S(1)} %collective-permute-done.22.refs_3_), custom_call_target="tpu_custom_call" | custom-call | flops 1000 | bytes 1000 | tf_op jit(solution)/shard_map/pallas_call | solution.py:455
  (18 shorter events, 0.1 us)
Async XLA Ops:
  0.6 12.3 %copy-start.1 = (bf16[1,1,256,512]{3,2,1,0:T(8,128)(2,1)S(1)}, bf16[1,1,256,512]{3,2,1,0:T(8,128)(2,1)}, u32[]{:S(2)}) copy-start(bf16[1,1,256,512]{3,2,1,0:T(8,128)(2,1)} %param.14) | copy-start | bytes 786436
  0.6 11.2 %copy-start.2 = (bf16[1,1,256,512]{3,2,1,0:T(8,128)(2,1)S(1)}, bf16[1,1,256,512]{3,2,1,0:T(8,128)(2,1)}, u32[]{:S(2)}) copy-start(bf16[1,1,256,512]{3,2,1,0:T(8,128)(2,1)} %param.15) | copy-start | bytes 786436
  0.7 12.3 %copy-start = (bf16[1,1,128,512]{3,2,1,0:T(8,128)(2,1)S(1)}, bf16[1,1,128,512]{3,2,1,0:T(8,128)(2,1)}, u32[]{:S(2)}) copy-start(bf16[1,1,128,512]{3,2,1,0:T(8,128)(2,1)} %param.12) | copy-start | bytes 393220
  0.7 12.3 %copy-start.3 = (s32[1,1,2]{2,1,0:T(1,128)S(1)}, s32[1,1,2]{2,1,0:T(1,128)}, u32[]{:S(2)}) copy-start(s32[1,1,2]{2,1,0:T(1,128)} %param.21) | copy-start | bytes 28
  0.7 10.5 %collective-permute-start.4 = (bf16[256,512]{1,0:T(8,128)(2,1)}, bf16[256,512]{1,0:T(8,128)(2,1)S(1)}, u32[]{:S(2)}, u32[]{:S(2)}) collective-permute-start(bf16[256,512]{1,0:T(8,128)(2,1)} %bitcast.18), channel_id=1, source_target_pairs={{0,16},{8,24},{16,0},{24,8},{1,17},{9,25},{17,1},{25,9},{2,18},{10... | collective-permute-start | bytes 786440 | tf_op jit(solution)/shard_map/ppermute | solution.py:298
  3.7 7.4 %collective-permute-start.5 = (bf16[256,512]{1,0:T(8,128)(2,1)}, bf16[256,512]{1,0:T(8,128)(2,1)S(1)}, u32[]{:S(2)}, u32[]{:S(2)}) collective-permute-start(bf16[256,512]{1,0:T(8,128)(2,1)} %bitcast.19), channel_id=1, source_target_pairs={{0,8},{8,0},{16,24},{24,16},{1,9},{9,1},{17,25},{25,17},{2,10},{10... | collective-permute-start | bytes 786440 | tf_op jit(solution)/shard_map/ppermute | solution.py:298
  5.7 5.2 %collective-permute-start.1 = (s32[8,128]{1,0:T(8,128)S(1)}, s32[8,128]{1,0:T(8,128)S(1)}, u32[]{:S(2)}, u32[]{:S(2)}) collective-permute-start(s32[8,128]{1,0:T(8,128)S(1)} %shard_map.162.info_ref.refs_0_), channel_id=1, source_target_pairs={{0,8},{8,0},{16,24},{24,16},{1,9},{9,1},{17,25},{25,17},{2,10},{10... | collective-permute-start | bytes 12296 | tf_op jit(solution)/shard_map/ppermute | solution.py:298
  6.2 4.9 %collective-permute-start = (s32[8,128]{1,0:T(8,128)S(1)}, s32[8,128]{1,0:T(8,128)S(1)}, u32[]{:S(2)}, u32[]{:S(2)}) collective-permute-start(s32[8,128]{1,0:T(8,128)S(1)} %shard_map.162.info_ref.refs_0_), channel_id=1, source_target_pairs={{0,16},{8,24},{16,0},{24,8},{1,17},{9,25},{17,1},{25,9},{2,18},{10... | collective-permute-start | bytes 12296 | tf_op jit(solution)/shard_map/ppermute | solution.py:298
  6.3 9.6 %collective-permute-start.3 = (bf16[256,512]{1,0:T(8,128)(2,1)}, bf16[256,512]{1,0:T(8,128)(2,1)S(1)}, u32[]{:S(2)}, u32[]{:S(2)}) collective-permute-start(bf16[256,512]{1,0:T(8,128)(2,1)} %bitcast.21), channel_id=1, source_target_pairs={{0,16},{8,24},{16,0},{24,8},{1,17},{9,25},{17,1},{25,9},{2,18},{10... | collective-permute-start | bytes 786440 | tf_op jit(solution)/shard_map/ppermute | solution.py:298
  11.2 1.7 %collective-permute-start.7 = (bf16[128,512]{1,0:T(8,128)(2,1)S(1)}, bf16[128,512]{1,0:T(8,128)(2,1)S(1)}, u32[]{:S(2)}, u32[]{:S(2)}) collective-permute-start(bf16[128,512]{1,0:T(8,128)(2,1)S(1)} %get-tuple-element.73), channel_id=1, source_target_pairs={{0,8},{8,0},{16,24},{24,16},{1,9},{9,1},{17,25},{25,17},{2,10},{10... | collective-permute-start | bytes 393224 | tf_op jit(solution)/shard_map/ppermute | solution.py:298
  11.3 1.7 %collective-permute-start.6 = (bf16[128,512]{1,0:T(8,128)(2,1)S(1)}, bf16[128,512]{1,0:T(8,128)(2,1)S(1)}, u32[]{:S(2)}, u32[]{:S(2)}) collective-permute-start(bf16[128,512]{1,0:T(8,128)(2,1)S(1)} %get-tuple-element.74), channel_id=1, source_target_pairs={{0,8},{8,0},{16,24},{24,16},{1,9},{9,1},{17,25},{25,17},{2,10},{10... | collective-permute-start | bytes 393224 | tf_op jit(solution)/shard_map/ppermute | solution.py:298
  11.7 1.2 %collective-permute-start.2 = (s32[8,128]{1,0:T(8,128)S(1)}, s32[8,128]{1,0:T(8,128)S(1)}, u32[]{:S(2)}, u32[]{:S(2)}) collective-permute-start(s32[8,128]{1,0:T(8,128)S(1)} %collective-permute-done.refs_1_), channel_id=1, source_target_pairs={{0,8},{8,0},{16,24},{24,16},{1,9},{9,1},{17,25},{25,17},{2,10},{10... | collective-permute-start | bytes 12296 | tf_op jit(solution)/shard_map/ppermute | solution.py:298
  11.8 5.9 %collective-permute-start.8 = (bf16[256,512]{1,0:T(8,128)(2,1)S(1)}, bf16[256,512]{1,0:T(8,128)(2,1)S(1)}, u32[]{:S(2)}, u32[]{:S(2)}) collective-permute-start(bf16[256,512]{1,0:T(8,128)(2,1)S(1)} %bitcast.22), channel_id=1, source_target_pairs={{0,8},{8,0},{16,24},{24,16},{1,9},{9,1},{17,25},{25,17},{2,10},{10... | collective-permute-start | bytes 786440 | tf_op jit(solution)/shard_map/ppermute | solution.py:298
  15.9 1.8 %collective-permute-start.9 = (bf16[256,512]{1,0:T(8,128)(2,1)S(1)}, bf16[256,512]{1,0:T(8,128)(2,1)S(1)}, u32[]{:S(2)}, u32[]{:S(2)}) collective-permute-start(bf16[256,512]{1,0:T(8,128)(2,1)S(1)} %collective-permute-done.3.refs_5_), channel_id=1, source_target_pairs={{0,8},{8,0},{16,24},{24,16},{1,9},{9,1},{17,25},{25,17},{2,10},{10... | collective-permute-start | bytes 786440 | tf_op jit(solution)/shard_map/ppermute | solution.py:298
  15.9 15.9 %collective-permute-start.17 = (bf16[256,512]{1,0:T(8,128)(2,1)S(1)}, bf16[256,512]{1,0:T(8,128)(2,1)S(1)}, u32[]{:S(2)}, u32[]{:S(2)}) collective-permute-start(bf16[256,512]{1,0:T(8,128)(2,1)S(1)} %get-tuple-element.66.refs_4_), channel_id=1, source_target_pairs={{0,16},{8,24},{16,0},{24,8},{1,17},{9,25},{17,1},{25,9},{2,18},{10... | collective-permute-start | bytes 786440 | tf_op jit(solution)/shard_map/ppermute | solution.py:298
  19.9 3.7 %collective-permute-start.10 = (f32[24,128]{1,0:T(8,128)S(1)}, f32[24,128]{1,0:T(8,128)S(1)}, u32[]{:S(2)}, u32[]{:S(2)}) collective-permute-start(f32[24,128]{1,0:T(8,128)S(1)} %get-tuple-element.53), channel_id=1, source_target_pairs={{0,1},{1,0},{2,3},{3,2},{4,5},{5,4},{6,7},{7,6},{8,9},{9,8},{10,11... | collective-permute-start | bytes 36872 | tf_op jit(solution)/shard_map/ppermute | solution.py:305
  22.0 10.5 %collective-permute-start.11 = (bf16[256,512]{1,0:T(8,128)(2,1)S(1)}, bf16[256,512]{1,0:T(8,128)(2,1)S(1)}, u32[]{:S(2)}, u32[]{:S(2)}) collective-permute-start(bf16[256,512]{1,0:T(8,128)(2,1)S(1)} %shard_map.166.refs_4_), channel_id=1, source_target_pairs={{0,16},{8,24},{16,0},{24,8},{1,17},{9,25},{17,1},{25,9},{2,18},{10... | collective-permute-start | bytes 786440 | tf_op jit(solution)/shard_map/ppermute | solution.py:298
  23.7 6.1 %collective-permute-start.14 = (f32[24,128]{1,0:T(8,128)S(1)}, f32[24,128]{1,0:T(8,128)S(1)}, u32[]{:S(2)}, u32[]{:S(2)}) collective-permute-start(f32[24,128]{1,0:T(8,128)S(1)} %add.12), channel_id=1, source_target_pairs={{0,6},{1,7},{2,4},{3,5},{4,2},{5,3},{6,0},{7,1},{8,14},{9,15},{10,... | collective-permute-start | bytes 36872 | tf_op jit(solution)/shard_map/ppermute | solution.py:305
  27.3 4.6 %collective-permute-start.13 = (f32[24,128]{1,0:T(8,128)S(1)}, f32[24,128]{1,0:T(8,128)S(1)}, u32[]{:S(2)}, u32[]{:S(2)}) collective-permute-start(f32[24,128]{1,0:T(8,128)S(1)} %add.12), channel_id=1, source_target_pairs={{0,4},{1,5},{2,6},{3,7},{4,0},{5,1},{6,2},{7,3},{8,12},{9,13},{10,... | collective-permute-start | bytes 36872 | tf_op jit(solution)/shard_map/ppermute | solution.py:305
  27.3 4.6 %collective-permute-start.12 = (f32[24,128]{1,0:T(8,128)S(1)}, f32[24,128]{1,0:T(8,128)S(1)}, u32[]{:S(2)}, u32[]{:S(2)}) collective-permute-start(f32[24,128]{1,0:T(8,128)S(1)} %add.12), channel_id=1, source_target_pairs={{0,2},{1,3},{2,0},{3,1},{4,6},{5,7},{6,4},{7,5},{8,10},{9,11},{10,... | collective-permute-start | bytes 36872 | tf_op jit(solution)/shard_map/ppermute | solution.py:305
  29.8 4.3 %collective-permute-start.18 = (bf16[256,512]{1,0:T(8,128)(2,1)S(1)}, bf16[256,512]{1,0:T(8,128)(2,1)S(1)}, u32[]{:S(2)}, u32[]{:S(2)}) collective-permute-start(bf16[256,512]{1,0:T(8,128)(2,1)S(1)} %get-tuple-element.66.refs_4_), channel_id=1, source_target_pairs={{0,8},{8,0},{16,24},{24,16},{1,9},{9,1},{17,25},{25,17},{2,10},{10... | collective-permute-start | bytes 786440 | tf_op jit(solution)/shard_map/ppermute | solution.py:298
  31.9 2.7 %collective-permute-start.19 = (bf16[256,512]{1,0:T(8,128)(2,1)S(1)}, bf16[256,512]{1,0:T(8,128)(2,1)S(1)}, u32[]{:S(2)}, u32[]{:S(2)}) collective-permute-start(bf16[256,512]{1,0:T(8,128)(2,1)S(1)} %collective-permute-done.17.refs_5_), channel_id=1, source_target_pairs={{0,8},{8,0},{16,24},{24,16},{1,9},{9,1},{17,25},{25,17},{2,10},{10... | collective-permute-start | bytes 786440 | tf_op jit(solution)/shard_map/ppermute | solution.py:298
  32.0 3.6 %collective-permute-start.15 = (bf16[256,512]{1,0:T(8,128)(2,1)S(1)}, bf16[256,512]{1,0:T(8,128)(2,1)S(1)}, u32[]{:S(2)}, u32[]{:S(2)}) collective-permute-start(bf16[256,512]{1,0:T(8,128)(2,1)S(1)} %shard_map.166.refs_4_), channel_id=1, source_target_pairs={{0,8},{8,0},{16,24},{24,16},{1,9},{9,1},{17,25},{25,17},{2,10},{10... | collective-permute-start | bytes 786440 | tf_op jit(solution)/shard_map/ppermute | solution.py:298
  32.5 3.1 %collective-permute-start.16 = (bf16[256,512]{1,0:T(8,128)(2,1)S(1)}, bf16[256,512]{1,0:T(8,128)(2,1)S(1)}, u32[]{:S(2)}, u32[]{:S(2)}) collective-permute-start(bf16[256,512]{1,0:T(8,128)(2,1)S(1)} %collective-permute-done.11.refs_5_), channel_id=1, source_target_pairs={{0,8},{8,0},{16,24},{24,16},{1,9},{9,1},{17,25},{25,17},{2,10},{10... | collective-permute-start | bytes 786440 | tf_op jit(solution)/shard_map/ppermute | solution.py:298
  32.5 3.9 %collective-permute-start.22 = (f32[24,128]{1,0:T(8,128)S(1)}, f32[24,128]{1,0:T(8,128)S(1)}, u32[]{:S(2)}, u32[]{:S(2)}) collective-permute-start(f32[24,128]{1,0:T(8,128)S(1)} %add_add_fusion.refs_0_), channel_id=1, source_target_pairs={{0,24},{1,25},{2,26},{3,27},{4,28},{5,29},{6,30},{7,31},{8,16},{9,... | collective-permute-start | bytes 36872 | tf_op jit(solution)/shard_map/ppermute | solution.py:305
  34.0 3.7 %collective-permute-start.21 = (f32[24,128]{1,0:T(8,128)S(1)}, f32[24,128]{1,0:T(8,128)S(1)}, u32[]{:S(2)}, u32[]{:S(2)}) collective-permute-start(f32[24,128]{1,0:T(8,128)S(1)} %add_add_fusion.refs_0_), channel_id=1, source_target_pairs={{0,16},{1,17},{2,18},{3,19},{4,20},{5,21},{6,22},{7,23},{8,24},{9,... | collective-permute-start | bytes 36872 | tf_op jit(solution)/shard_map/ppermute | solution.py:305
  34.6 3.1 %collective-permute-start.20 = (f32[24,128]{1,0:T(8,128)S(1)}, f32[24,128]{1,0:T(8,128)S(1)}, u32[]{:S(2)}, u32[]{:S(2)}) collective-permute-start(f32[24,128]{1,0:T(8,128)S(1)} %add_add_fusion.refs_0_), channel_id=1, source_target_pairs={{0,8},{1,9},{2,10},{3,11},{4,12},{5,13},{6,14},{7,15},{8,0},{9,1},... | collective-permute-start | bytes 36872 | tf_op jit(solution)/shard_map/ppermute | solution.py:305
where the time goes:
time: 38.5 us; the launch traced here: 38.3 us
  starting transfers between devices  18.6 us (48%)
  Pallas kernels  12.1 us (31%)
  waiting for transfers between devices  4.85 us (13%)
  between operations  2.71 us (7%)
    ppermute x16, starting transfers between devices, shifted(): return lax.ppermute(x, axis, pairs)  10.6 us
    ppermute x7, starting transfers between devices, step_terms(): lax.ppermute(x, ('resp', 'dp'), [(i, i ^ flip) for i in range(count)])  7.98 us
    ppermute x7, waiting for transfers between devices, step_terms(): lax.ppermute(x, ('resp', 'dp'), [(i, i ^ flip) for i in range(count)])  3.56 us
    pallas_call x1, Pallas kernels, per_device(): call(functools.partial(self_kernel, kv_heads, gsize), [shape((kv_heads, g...  2.67 us
    pallas_call x1, Pallas kernels, per_device(): call(functools.partial(prob_kernel, kv_heads, gsize, count, len(keys_near...  2.57 us
    pallas_call x1, Pallas kernels, per_device(): call(functools.partial(score_kernel, kv_heads, gsize, count), [shape((kv_...  2.17 us
    pallas_call x2, Pallas kernels, summed(): call(functools.partial(sum_kernel, count), [shape((prefix_len, width_kv),...  1.83 us
    pallas_call x1, Pallas kernels, per_device(): call(functools.partial(grad_kernel, kv_heads, gsize), [shape((rows, width...  1.71 us
  transfers between devices with their start and end apart: 23, of which 6 were waited for; matrix products, arithmetic and copies ran while one was open for 0% of the time, Pallas kernels for 30%

commit v1 on v0

--- a/solution.py
+++ b/solution.py
@@ -432,7 +432,6 @@
     devices = holders * batches
     bits = [1 << i for i in range(devices.bit_length() - 1)]
     dp_bits = [bit for bit in bits if bit < batches]
-    core_bits = [bit for bit in bits if batches <= bit < batches * cores]
     y_bits = [bit for bit in bits if bit >= batches * cores]
     share = step_sum(share, dp_bits[:1], devices, dkey_pre)
 
@@ -449,9 +448,9 @@
     dkeys_across = after(dkeys_across, (share, key_grad))
     prefix_key_grad = summed(dkey_pre, *dkeys_across, *dkeys_core, *to_core(dkeys_across))
 
-    for bit in y_bits[1:]:
+    for bit in y_bits:
         share = step_sum(share, [bit], devices, prefix_value_grad)
-    shares = after(step_terms(share, core_bits + y_bits[:1], devices), (prefix_value_grad, prefix_key_grad))
+    shares = [share, *after(to_core([share]), prefix_key_grad)]
     q_total, v_total = call(
         functools.partial(last_kernel, devices),
         [shape((kv_heads * gsize, HEAD_DIM), f32), shape((kv_heads, HEAD_DIM), f32)],

time: 38.5 us -> 38.2 us (level)
  starting transfers between devices: 18.6 us -> 18 us
    ppermute x7 -> x5, starting transfers between devices: 7.98 us -> 7.34 us  [step_terms(): lax.ppermute(x, ('resp', 'dp'), [(i, i ^ flip) for i in range(count)])]
    ppermute x16 -> x17, waiting for transfers between devices: 1.29 us -> 1.53 us  [shifted(): return lax.ppermute(x, axis, pairs)]
    ppermute x7 -> x5, waiting for transfers between devices: 3.56 us -> 3.63 us  [step_terms(): lax.ppermute(x, ('resp', 'dp'), [(i, i ^ flip) for i in range(count)])]
    ppermute x16 -> x17, starting transfers between devices: 10.6 us -> 10.6 us  [shifted(): return lax.ppermute(x, axis, pairs)]
  transfers between devices with their start and end apart: 23 -> 22, of which waited for: 6 -> 7; matrix products, arithmetic and copies ran while one was open for 0% -> 0% of each run, Pallas kernels for 30% -> 30%
where the time goes in v1:
time: 38.2 us; the launch traced here: 38 us
  starting transfers between devices  18 us (47%)
  Pallas kernels  12.1 us (32%)
  waiting for transfers between devices  5.17 us (14%)
  between operations  2.72 us (7%)
    ppermute x17, starting transfers between devices, shifted(): return lax.ppermute(x, axis, pairs)  10.6 us
    ppermute x5, starting transfers between devices, step_terms(): lax.ppermute(x, ('resp', 'dp'), [(i, i ^ flip) for i in range(count)])  7.34 us
    ppermute x5, waiting for transfers between devices, step_terms(): lax.ppermute(x, ('resp', 'dp'), [(i, i ^ flip) for i in range(count)])  3.63 us
    pallas_call x1, Pallas kernels, per_device(): call(functools.partial(self_kernel, kv_heads, gsize), [shape((kv_heads, g...  2.67 us
    pallas_call x1, Pallas kernels, per_device(): call(functools.partial(prob_kernel, kv_heads, gsize, count, len(keys_near...  2.57 us
    pallas_call x1, Pallas kernels, per_device(): call(functools.partial(score_kernel, kv_heads, gsize, count), [shape((kv_...  2.17 us
    pallas_call x2, Pallas kernels, summed(): call(functools.partial(sum_kernel, count), [shape((prefix_len, width_kv),...  1.83 us
    pallas_call x1, Pallas kernels, per_device(): call(functools.partial(grad_kernel, kv_heads, gsize), [shape((rows, width...  1.71 us
  transfers between devices with their start and end apart: 22, of which 7 were waited for; matrix products, arithmetic and copies ran while one was open for 0% of the time, Pallas kernels for 30%

profile of v1, /device:TPU:0, one launch (start us, length us, event | category | flops | bytes accessed | tf_op | source)
XLA Modules:
  0.0 38.0 jit_solution(16979644840200039264)
XLA Ops:
  0.6 0.0 copy-start.2
  0.7 0.0 copy-start
  0.7 3.0 %collective-permute-start.4 = (bf16[256,512]{1,0:T(8,128)(2,1)}, bf16[256,512]{1,0:T(8,128)(2,1)S(1)}, u32[]{:S(2)}, u32[]{:S(2)}) collective-permute-start(bf16[256,512]{1,0:T(8,128)(2,1)} %bitcast.18), channel_id=1, source_target_pairs={{0,16},{8,24},{16,0},{24,8},{1,17},{9,25},{17,1},{25,9},{2,18},{10... | collective-permute-start | bytes 786440 | tf_op jit(solution)/shard_map/ppermute | solution.py:298
  3.7 0.0 collective-permute-start.5
  5.7 0.1 shard_map.162.info_ref.refs_0_
  5.7 0.5 %collective-permute-start.1 = (s32[8,128]{1,0:T(8,128)S(1)}, s32[8,128]{1,0:T(8,128)S(1)}, u32[]{:S(2)}, u32[]{:S(2)}) collective-permute-start(s32[8,128]{1,0:T(8,128)S(1)} %shard_map.162.info_ref.refs_0_), channel_id=1, source_target_pairs={{0,8},{8,0},{16,24},{24,16},{1,9},{9,1},{17,25},{25,17},{2,10},{10... | collective-permute-start | bytes 12296 | tf_op jit(solution)/shard_map/ppermute | solution.py:298
  6.2 0.1 collective-permute-start
  6.3 1.9 %collective-permute-start.3 = (bf16[256,512]{1,0:T(8,128)(2,1)}, bf16[256,512]{1,0:T(8,128)(2,1)S(1)}, u32[]{:S(2)}, u32[]{:S(2)}) collective-permute-start(bf16[256,512]{1,0:T(8,128)(2,1)} %bitcast.21), channel_id=1, source_target_pairs={{0,16},{8,24},{16,0},{24,8},{1,17},{9,25},{17,1},{25,9},{2,18},{10... | collective-permute-start | bytes 786440 | tf_op jit(solution)/shard_map/ppermute | solution.py:298
  8.3 2.7 %shard_map.163 = (bf16[4,640,128]{2,1,0:T(8,128)(2,1)S(1)}, bf16[4,640,128]{2,1,0:T(8,128)(2,1)S(1)}, f32[4,128,640]{2,1,0:T(8,128)S(1)}, f32[4,128,640]{2,1,0:T(8,128)S(1)}) custom-call(s32[8,128]{1,0:T(8,128)S(1)} %shard_map.162.info_ref.refs_0_, bf16[20,128]{1,0:T(8,128)(2,1)} %bitcast.30, bf16[128,512]{1,0:T(8,128)(2,1)} %bitcast.16, ...), custom_call_target="tpu_custom_call" | custom-call | flops 1000 | bytes 1000 | tf_op jit(solution)/shard_map/pallas_call | solution.py:366
  10.9 0.0 collective-permute-done.1.refs_2_
  11.0 0.2 collective-permute-done.refs_1_
  11.1 0.0 collective-permute-done.4.refs_5_
  11.1 0.0 collective-permute-done.5.refs_6_
  11.2 0.1 collective-permute-start.7
  11.3 0.5 %collective-permute-start.6 = (bf16[128,512]{1,0:T(8,128)(2,1)S(1)}, bf16[128,512]{1,0:T(8,128)(2,1)S(1)}, u32[]{:S(2)}, u32[]{:S(2)}) collective-permute-start(bf16[128,512]{1,0:T(8,128)(2,1)S(1)} %get-tuple-element.72), channel_id=1, source_target_pairs={{0,8},{8,0},{16,24},{24,16},{1,9},{9,1},{17,25},{25,17},{2,10},{10... | collective-permute-start | bytes 393224 | tf_op jit(solution)/shard_map/ppermute | solution.py:298
  11.7 0.1 collective-permute-start.2
  11.8 0.4 %collective-permute-start.8 = (bf16[256,512]{1,0:T(8,128)(2,1)S(1)}, bf16[256,512]{1,0:T(8,128)(2,1)S(1)}, u32[]{:S(2)}, u32[]{:S(2)}) collective-permute-start(bf16[256,512]{1,0:T(8,128)(2,1)S(1)} %bitcast.22), channel_id=1, source_target_pairs={{0,8},{8,0},{16,24},{24,16},{1,9},{9,1},{17,25},{25,17},{2,10},{10... | collective-permute-start | bytes 786440 | tf_op jit(solution)/shard_map/ppermute | solution.py:298
  12.3 0.7 %collective-permute-done.2.refs_3_ = s32[8,128]{1,0:T(8,128)S(1)} collective-permute-done((s32[8,128]{1,0:T(8,128)S(1)}, s32[8,128]{1,0:T(8,128)S(1)}, u32[]{:S(2)}, u32[]{:S(2)}) %collective-permute-start.2) | collective-permute-done | bytes 4128 | tf_op jit(solution)/shard_map/ppermute | solution.py:298
  12.9 0.0 collective-permute-done.7.refs_8_
  12.9 0.0 collective-permute-done.6.refs_7_
  12.9 2.6 %shard_map.164 = (bf16[384,512]{1,0:T(8,128)(2,1)S(1)}, bf16[4,384,640]{2,1,0:T(8,128)(2,1)S(1)}, bf16[256,512]{1,0:T(8,128)(2,1)S(1)}, bf16[128,512]{1,0:T(8,128)(2,1)}, f32[4,128]{1,0:T(4,128)S(1)}) custom-call(s32[8,128]{1,0:T(8,128)S(1)} %shard_map.162.info_ref.refs_0_, s32[8,128]{1,0:T(8,128)S(1)} %collective-permute-done.refs_1_, ...), custom_call_target="tpu_custom_call" | custom-call | flops 1000 | bytes 1000 | tf_op jit(solution)/shard_map/pallas_call | solution.py:397
  15.5 0.4 %collective-permute-done.3.refs_5_ = bf16[256,512]{1,0:T(8,128)(2,1)S(1)} collective-permute-done((bf16[256,512]{1,0:T(8,128)(2,1)}, bf16[256,512]{1,0:T(8,128)(2,1)S(1)}, u32[]{:S(2)}, u32[]{:S(2)}) %collective-permute-start.3) | collective-permute-done | bytes 262176 | tf_op jit(solution)/shard_map/ppermute | solution.py:298
  15.9 0.0 collective-permute-start.9
  15.9 1.8 %collective-permute-start.17 = (bf16[256,512]{1,0:T(8,128)(2,1)S(1)}, bf16[256,512]{1,0:T(8,128)(2,1)S(1)}, u32[]{:S(2)}, u32[]{:S(2)}) collective-permute-start(bf16[256,512]{1,0:T(8,128)(2,1)S(1)} %get-tuple-element.65.refs_4_), channel_id=1, source_target_pairs={{0,16},{8,24},{16,0},{24,8},{1,17},{9,25},{17,1},{25,9},{2,18},{10... | collective-permute-start | bytes 786440 | tf_op jit(solution)/shard_map/ppermute | solution.py:298
  17.8 0.0 collective-permute-done.8.refs_6_
  17.8 2.2 %shard_map.165 = (bf16[4,384,640]{2,1,0:T(8,128)(2,1)S(1)}, f32[24,128]{1,0:T(8,128)S(1)}) custom-call(s32[8,128]{1,0:T(8,128)S(1)} %shard_map.162.info_ref.refs_0_, s32[8,128]{1,0:T(8,128)S(1)} %collective-permute-done.refs_1_, s32[8,128]{1,0:T(8,128)S(1)} %collective-permute-done.1.refs_2_, s32[8,128]{1,0:T(8,128)S(1)} %collective-permute-done.2.refs_3_, ...), custom_call_target="tpu_custom_call" | custom-call | flops 1000 | bytes 1000 | tf_op jit(solution)/shard_map/pallas_call | solution.py:413
  19.9 1.5 %collective-permute-start.10 = (f32[24,128]{1,0:T(8,128)S(1)}, f32[24,128]{1,0:T(8,128)S(1)}, u32[]{:S(2)}, u32[]{:S(2)}) collective-permute-start(f32[24,128]{1,0:T(8,128)S(1)} %get-tuple-element.52), channel_id=1, source_target_pairs={{0,1},{1,0},{2,3},{3,2},{4,5},{5,4},{6,7},{7,6},{8,9},{9,8},{10,11... | collective-permute-start | bytes 36872 | tf_op jit(solution)/shard_map/ppermute | solution.py:305
  21.5 0.5 %shard_map.166.refs_4_ = bf16[256,512]{1,0:T(8,128)(2,1)S(1)} custom-call(bf16[4,384,640]{2,1,0:T(8,128)(2,1)S(1)} %get-tuple-element.54.ds_ref, bf16[4,640,128]{2,1,0:T(8,128)(2,1)S(1)} %get-tuple-element.43.refs_10_.qs_ref), custom_call_target="tpu_custom_call" | custom-call | flops 1000 | bytes 1000 | tf_op jit(solution)/shard_map/pallas_call | solution.py:425
  22.0 1.5 %collective-permute-start.11 = (bf16[256,512]{1,0:T(8,128)(2,1)S(1)}, bf16[256,512]{1,0:T(8,128)(2,1)S(1)}, u32[]{:S(2)}, u32[]{:S(2)}) collective-permute-start(bf16[256,512]{1,0:T(8,128)(2,1)S(1)} %shard_map.166.refs_4_), channel_id=1, source_target_pairs={{0,16},{8,24},{16,0},{24,8},{1,17},{9,25},{17,1},{25,9},{2,18},{10... | collective-permute-start | bytes 786440 | tf_op jit(solution)/shard_map/ppermute | solution.py:298
  23.5 0.2 collective-permute-done.10
  23.7 3.6 %collective-permute-start.14 = (f32[24,128]{1,0:T(8,128)S(1)}, f32[24,128]{1,0:T(8,128)S(1)}, u32[]{:S(2)}, u32[]{:S(2)}) collective-permute-start(f32[24,128]{1,0:T(8,128)S(1)} %add.15), channel_id=1, source_target_pairs={{0,6},{1,7},{2,4},{3,5},{4,2},{5,3},{6,0},{7,1},{8,14},{9,15},{10,... | collective-permute-start | bytes 36872 | tf_op jit(solution)/shard_map/ppermute | solution.py:305
  27.3 0.0 collective-permute-start.13
  27.3 0.8 %collective-permute-start.12 = (f32[24,128]{1,0:T(8,128)S(1)}, f32[24,128]{1,0:T(8,128)S(1)}, u32[]{:S(2)}, u32[]{:S(2)}) collective-permute-start(f32[24,128]{1,0:T(8,128)S(1)} %add.15), channel_id=1, source_target_pairs={{0,2},{1,3},{2,0},{3,1},{4,6},{5,7},{6,4},{7,5},{8,10},{9,11},{10,... | collective-permute-start | bytes 36872 | tf_op jit(solution)/shard_map/ppermute | solution.py:305
  28.0 1.7 %shard_map.167 = (bf16[128,2560]{1,0:T(8,128)(2,1)}, bf16[128,512]{1,0:T(8,128)(2,1)}) custom-call(bf16[4,384,640]{2,1,0:T(8,128)(2,1)S(1)} %get-tuple-element.54.ds_ref, bf16[384,512]{1,0:T(8,128)(2,1)S(1)} %get-tuple-element.49.refs_11_.ka_ref, bf16[4,640,128]{2,1,0:T(8,128)(2,1)S(1)} %get-tuple-element.43.refs_10_.qs_ref), custom_call_target="tpu_custom_call" | custom-call | flops 1000 | bytes 1000 | tf_op jit(solution)/shard_map/pallas_call | solution.py:438
  29.8 2.1 %collective-permute-done.13 = f32[24,128]{1,0:T(8,128)S(1)} collective-permute-done((f32[24,128]{1,0:T(8,128)S(1)}, f32[24,128]{1,0:T(8,128)S(1)}, u32[]{:S(2)}, u32[]{:S(2)}) %collective-permute-start.13) | collective-permute-done | bytes 12320 | tf_op jit(solution)/shard_map/ppermute | solution.py:305
  31.9 0.0 collective-permute-done.12
  31.9 0.1 collective-permute-start.19
  32.0 0.5 %collective-permute-start.15 = (bf16[256,512]{1,0:T(8,128)(2,1)S(1)}, bf16[256,512]{1,0:T(8,128)(2,1)S(1)}, u32[]{:S(2)}, u32[]{:S(2)}) collective-permute-start(bf16[256,512]{1,0:T(8,128)(2,1)S(1)} %shard_map.166.refs_4_), channel_id=1, source_target_pairs={{0,8},{8,0},{16,24},{24,16},{1,9},{9,1},{17,25},{25,17},{2,10},{10... | collective-permute-start | bytes 786440 | tf_op jit(solution)/shard_map/ppermute | solution.py:298
  32.5 0.1 collective-permute-start.16
  32.5 1.4 %collective-permute-start.20 = (f32[24,128]{1,0:T(8,128)S(1)}, f32[24,128]{1,0:T(8,128)S(1)}, u32[]{:S(2)}, u32[]{:S(2)}) collective-permute-start(f32[24,128]{1,0:T(8,128)S(1)} %add_add_fusion), channel_id=1, source_target_pairs={{0,16},{1,17},{2,18},{3,19},{4,20},{5,21},{6,22},{7,23},{8,24},{9,... | collective-permute-start | bytes 36872 | tf_op jit(solution)/shard_map/ppermute | solution.py:305
  34.0 0.0 collective-permute-done.18.refs_6_
  34.0 0.9 %shard_map.169 = bf16[256,512]{1,0:T(8,128)(2,1)} custom-call(s32[8,128]{1,0:T(8,128)S(1)} %shard_map.162.info_ref.refs_0_, s32[8,128]{1,0:T(8,128)S(1)} %collective-permute-done.refs_1_, s32[8,128]{1,0:T(8,128)S(1)} %collective-permute-done.1.refs_2_, s32[8,128]{1,0:T(8,128)S(1)} %collective-permute-done.2.refs_3_, ...), custom_call_target="tpu_custom_call" | custom-call | flops 1000 | bytes 1000 | tf_op jit(solution)/shard_map/pallas_call | solution.py:346
  34.9 1.3 %collective-permute-done.20 = f32[24,128]{1,0:T(8,128)S(1)} collective-permute-done((f32[24,128]{1,0:T(8,128)S(1)}, f32[24,128]{1,0:T(8,128)S(1)}, u32[]{:S(2)}, u32[]{:S(2)}) %collective-permute-start.20) | collective-permute-done | bytes 12320 | tf_op jit(solution)/shard_map/ppermute | solution.py:305
  36.2 0.0 collective-permute-start.21
  36.2 0.0 collective-permute-done.15.refs_6_
  36.3 0.9 %shard_map.168 = bf16[256,512]{1,0:T(8,128)(2,1)} custom-call(s32[8,128]{1,0:T(8,128)S(1)} %shard_map.162.info_ref.refs_0_, s32[8,128]{1,0:T(8,128)S(1)} %collective-permute-done.refs_1_, s32[8,128]{1,0:T(8,128)S(1)} %collective-permute-done.1.refs_2_, s32[8,128]{1,0:T(8,128)S(1)} %collective-permute-done.2.refs_3_, ...), custom_call_target="tpu_custom_call" | custom-call | flops 1000 | bytes 1000 | tf_op jit(solution)/shard_map/pallas_call | solution.py:346
  37.2 0.2 collective-permute-done.21.refs_1_
  37.4 0.6 %shard_map.170 = (f32[20,128]{1,0:T(8,128)}, f32[4,128]{1,0:T(4,128)}) custom-call(f32[24,128]{1,0:T(8,128)S(1)} %add.19.refs_0_, f32[24,128]{1,0:T(8,128)S(1)} %collective-permute-done.21.refs_1_), custom_call_target="tpu_custom_call" | custom-call | flops 1000 | bytes 1000 | tf_op jit(solution)/shard_map/pallas_call | solution.py:454
  (17 shorter events, 0.1 us)
Async XLA Ops:
  0.6 12.3 %copy-start.1 = (bf16[1,1,256,512]{3,2,1,0:T(8,128)(2,1)S(1)}, bf16[1,1,256,512]{3,2,1,0:T(8,128)(2,1)}, u32[]{:S(2)}) copy-start(bf16[1,1,256,512]{3,2,1,0:T(8,128)(2,1)} %param.14) | copy-start | bytes 786436
  0.6 11.2 %copy-start.2 = (bf16[1,1,256,512]{3,2,1,0:T(8,128)(2,1)S(1)}, bf16[1,1,256,512]{3,2,1,0:T(8,128)(2,1)}, u32[]{:S(2)}) copy-start(bf16[1,1,256,512]{3,2,1,0:T(8,128)(2,1)} %param.15) | copy-start | bytes 786436
  0.7 12.3 %copy-start = (bf16[1,1,128,512]{3,2,1,0:T(8,128)(2,1)S(1)}, bf16[1,1,128,512]{3,2,1,0:T(8,128)(2,1)}, u32[]{:S(2)}) copy-start(bf16[1,1,128,512]{3,2,1,0:T(8,128)(2,1)} %param.12) | copy-start | bytes 393220
  0.7 12.3 %copy-start.3 = (s32[1,1,2]{2,1,0:T(1,128)S(1)}, s32[1,1,2]{2,1,0:T(1,128)}, u32[]{:S(2)}) copy-start(s32[1,1,2]{2,1,0:T(1,128)} %param.21) | copy-start | bytes 28
  0.7 10.5 %collective-permute-start.4 = (bf16[256,512]{1,0:T(8,128)(2,1)}, bf16[256,512]{1,0:T(8,128)(2,1)S(1)}, u32[]{:S(2)}, u32[]{:S(2)}) collective-permute-start(bf16[256,512]{1,0:T(8,128)(2,1)} %bitcast.18), channel_id=1, source_target_pairs={{0,16},{8,24},{16,0},{24,8},{1,17},{9,25},{17,1},{25,9},{2,18},{10... | collective-permute-start | bytes 786440 | tf_op jit(solution)/shard_map/ppermute | solution.py:298
  3.7 7.4 %collective-permute-start.5 = (bf16[256,512]{1,0:T(8,128)(2,1)}, bf16[256,512]{1,0:T(8,128)(2,1)S(1)}, u32[]{:S(2)}, u32[]{:S(2)}) collective-permute-start(bf16[256,512]{1,0:T(8,128)(2,1)} %bitcast.19), channel_id=1, source_target_pairs={{0,8},{8,0},{16,24},{24,16},{1,9},{9,1},{17,25},{25,17},{2,10},{10... | collective-permute-start | bytes 786440 | tf_op jit(solution)/shard_map/ppermute | solution.py:298
  5.7 5.2 %collective-permute-start.1 = (s32[8,128]{1,0:T(8,128)S(1)}, s32[8,128]{1,0:T(8,128)S(1)}, u32[]{:S(2)}, u32[]{:S(2)}) collective-permute-start(s32[8,128]{1,0:T(8,128)S(1)} %shard_map.162.info_ref.refs_0_), channel_id=1, source_target_pairs={{0,8},{8,0},{16,24},{24,16},{1,9},{9,1},{17,25},{25,17},{2,10},{10... | collective-permute-start | bytes 12296 | tf_op jit(solution)/shard_map/ppermute | solution.py:298
  6.2 4.9 %collective-permute-start = (s32[8,128]{1,0:T(8,128)S(1)}, s32[8,128]{1,0:T(8,128)S(1)}, u32[]{:S(2)}, u32[]{:S(2)}) collective-permute-start(s32[8,128]{1,0:T(8,128)S(1)} %shard_map.162.info_ref.refs_0_), channel_id=1, source_target_pairs={{0,16},{8,24},{16,0},{24,8},{1,17},{9,25},{17,1},{25,9},{2,18},{10... | collective-permute-start | bytes 12296 | tf_op jit(solution)/shard_map/ppermute | solution.py:298
  6.3 9.6 %collective-permute-start.3 = (bf16[256,512]{1,0:T(8,128)(2,1)}, bf16[256,512]{1,0:T(8,128)(2,1)S(1)}, u32[]{:S(2)}, u32[]{:S(2)}) collective-permute-start(bf16[256,512]{1,0:T(8,128)(2,1)} %bitcast.21), channel_id=1, source_target_pairs={{0,16},{8,24},{16,0},{24,8},{1,17},{9,25},{17,1},{25,9},{2,18},{10... | collective-permute-start | bytes 786440 | tf_op jit(solution)/shard_map/ppermute | solution.py:298
  11.2 1.7 %collective-permute-start.7 = (bf16[128,512]{1,0:T(8,128)(2,1)S(1)}, bf16[128,512]{1,0:T(8,128)(2,1)S(1)}, u32[]{:S(2)}, u32[]{:S(2)}) collective-permute-start(bf16[128,512]{1,0:T(8,128)(2,1)S(1)} %get-tuple-element.71), channel_id=1, source_target_pairs={{0,8},{8,0},{16,24},{24,16},{1,9},{9,1},{17,25},{25,17},{2,10},{10... | collective-permute-start | bytes 393224 | tf_op jit(solution)/shard_map/ppermute | solution.py:298
  11.3 1.7 %collective-permute-start.6 = (bf16[128,512]{1,0:T(8,128)(2,1)S(1)}, bf16[128,512]{1,0:T(8,128)(2,1)S(1)}, u32[]{:S(2)}, u32[]{:S(2)}) collective-permute-start(bf16[128,512]{1,0:T(8,128)(2,1)S(1)} %get-tuple-element.72), channel_id=1, source_target_pairs={{0,8},{8,0},{16,24},{24,16},{1,9},{9,1},{17,25},{25,17},{2,10},{10... | collective-permute-start | bytes 393224 | tf_op jit(solution)/shard_map/ppermute | solution.py:298
  11.7 1.2 %collective-permute-start.2 = (s32[8,128]{1,0:T(8,128)S(1)}, s32[8,128]{1,0:T(8,128)S(1)}, u32[]{:S(2)}, u32[]{:S(2)}) collective-permute-start(s32[8,128]{1,0:T(8,128)S(1)} %collective-permute-done.refs_1_), channel_id=1, source_target_pairs={{0,8},{8,0},{16,24},{24,16},{1,9},{9,1},{17,25},{25,17},{2,10},{10... | collective-permute-start | bytes 12296 | tf_op jit(solution)/shard_map/ppermute | solution.py:298
  11.8 5.9 %collective-permute-start.8 = (bf16[256,512]{1,0:T(8,128)(2,1)S(1)}, bf16[256,512]{1,0:T(8,128)(2,1)S(1)}, u32[]{:S(2)}, u32[]{:S(2)}) collective-permute-start(bf16[256,512]{1,0:T(8,128)(2,1)S(1)} %bitcast.22), channel_id=1, source_target_pairs={{0,8},{8,0},{16,24},{24,16},{1,9},{9,1},{17,25},{25,17},{2,10},{10... | collective-permute-start | bytes 786440 | tf_op jit(solution)/shard_map/ppermute | solution.py:298
  15.9 1.8 %collective-permute-start.9 = (bf16[256,512]{1,0:T(8,128)(2,1)S(1)}, bf16[256,512]{1,0:T(8,128)(2,1)S(1)}, u32[]{:S(2)}, u32[]{:S(2)}) collective-permute-start(bf16[256,512]{1,0:T(8,128)(2,1)S(1)} %collective-permute-done.3.refs_5_), channel_id=1, source_target_pairs={{0,8},{8,0},{16,24},{24,16},{1,9},{9,1},{17,25},{25,17},{2,10},{10... | collective-permute-start | bytes 786440 | tf_op jit(solution)/shard_map/ppermute | solution.py:298
  15.9 15.9 %collective-permute-start.17 = (bf16[256,512]{1,0:T(8,128)(2,1)S(1)}, bf16[256,512]{1,0:T(8,128)(2,1)S(1)}, u32[]{:S(2)}, u32[]{:S(2)}) collective-permute-start(bf16[256,512]{1,0:T(8,128)(2,1)S(1)} %get-tuple-element.65.refs_4_), channel_id=1, source_target_pairs={{0,16},{8,24},{16,0},{24,8},{1,17},{9,25},{17,1},{25,9},{2,18},{10... | collective-permute-start | bytes 786440 | tf_op jit(solution)/shard_map/ppermute | solution.py:298
  19.9 3.7 %collective-permute-start.10 = (f32[24,128]{1,0:T(8,128)S(1)}, f32[24,128]{1,0:T(8,128)S(1)}, u32[]{:S(2)}, u32[]{:S(2)}) collective-permute-start(f32[24,128]{1,0:T(8,128)S(1)} %get-tuple-element.52), channel_id=1, source_target_pairs={{0,1},{1,0},{2,3},{3,2},{4,5},{5,4},{6,7},{7,6},{8,9},{9,8},{10,11... | collective-permute-start | bytes 36872 | tf_op jit(solution)/shard_map/ppermute | solution.py:305
  22.0 10.5 %collective-permute-start.11 = (bf16[256,512]{1,0:T(8,128)(2,1)S(1)}, bf16[256,512]{1,0:T(8,128)(2,1)S(1)}, u32[]{:S(2)}, u32[]{:S(2)}) collective-permute-start(bf16[256,512]{1,0:T(8,128)(2,1)S(1)} %shard_map.166.refs_4_), channel_id=1, source_target_pairs={{0,16},{8,24},{16,0},{24,8},{1,17},{9,25},{17,1},{25,9},{2,18},{10... | collective-permute-start | bytes 786440 | tf_op jit(solution)/shard_map/ppermute | solution.py:298
  23.7 6.1 %collective-permute-start.14 = (f32[24,128]{1,0:T(8,128)S(1)}, f32[24,128]{1,0:T(8,128)S(1)}, u32[]{:S(2)}, u32[]{:S(2)}) collective-permute-start(f32[24,128]{1,0:T(8,128)S(1)} %add.15), channel_id=1, source_target_pairs={{0,6},{1,7},{2,4},{3,5},{4,2},{5,3},{6,0},{7,1},{8,14},{9,15},{10,... | collective-permute-start | bytes 36872 | tf_op jit(solution)/shard_map/ppermute | solution.py:305
  27.3 4.6 %collective-permute-start.13 = (f32[24,128]{1,0:T(8,128)S(1)}, f32[24,128]{1,0:T(8,128)S(1)}, u32[]{:S(2)}, u32[]{:S(2)}) collective-permute-start(f32[24,128]{1,0:T(8,128)S(1)} %add.15), channel_id=1, source_target_pairs={{0,4},{1,5},{2,6},{3,7},{4,0},{5,1},{6,2},{7,3},{8,12},{9,13},{10,... | collective-permute-start | bytes 36872 | tf_op jit(solution)/shard_map/ppermute | solution.py:305
  27.3 4.6 %collective-permute-start.12 = (f32[24,128]{1,0:T(8,128)S(1)}, f32[24,128]{1,0:T(8,128)S(1)}, u32[]{:S(2)}, u32[]{:S(2)}) collective-permute-start(f32[24,128]{1,0:T(8,128)S(1)} %add.15), channel_id=1, source_target_pairs={{0,2},{1,3},{2,0},{3,1},{4,6},{5,7},{6,4},{7,5},{8,10},{9,11},{10,... | collective-permute-start | bytes 36872 | tf_op jit(solution)/shard_map/ppermute | solution.py:305
  29.8 4.2 %collective-permute-start.18 = (bf16[256,512]{1,0:T(8,128)(2,1)S(1)}, bf16[256,512]{1,0:T(8,128)(2,1)S(1)}, u32[]{:S(2)}, u32[]{:S(2)}) collective-permute-start(bf16[256,512]{1,0:T(8,128)(2,1)S(1)} %get-tuple-element.65.refs_4_), channel_id=1, source_target_pairs={{0,8},{8,0},{16,24},{24,16},{1,9},{9,1},{17,25},{25,17},{2,10},{10... | collective-permute-start | bytes 786440 | tf_op jit(solution)/shard_map/ppermute | solution.py:298
  31.9 2.1 %collective-permute-start.19 = (bf16[256,512]{1,0:T(8,128)(2,1)S(1)}, bf16[256,512]{1,0:T(8,128)(2,1)S(1)}, u32[]{:S(2)}, u32[]{:S(2)}) collective-permute-start(bf16[256,512]{1,0:T(8,128)(2,1)S(1)} %collective-permute-done.17.refs_5_), channel_id=1, source_target_pairs={{0,8},{8,0},{16,24},{24,16},{1,9},{9,1},{17,25},{25,17},{2,10},{10... | collective-permute-start | bytes 786440 | tf_op jit(solution)/shard_map/ppermute | solution.py:298
  32.0 4.3 %collective-permute-start.15 = (bf16[256,512]{1,0:T(8,128)(2,1)S(1)}, bf16[256,512]{1,0:T(8,128)(2,1)S(1)}, u32[]{:S(2)}, u32[]{:S(2)}) collective-permute-start(bf16[256,512]{1,0:T(8,128)(2,1)S(1)} %shard_map.166.refs_4_), channel_id=1, source_target_pairs={{0,8},{8,0},{16,24},{24,16},{1,9},{9,1},{17,25},{25,17},{2,10},{10... | collective-permute-start | bytes 786440 | tf_op jit(solution)/shard_map/ppermute | solution.py:298
  32.5 3.8 %collective-permute-start.16 = (bf16[256,512]{1,0:T(8,128)(2,1)S(1)}, bf16[256,512]{1,0:T(8,128)(2,1)S(1)}, u32[]{:S(2)}, u32[]{:S(2)}) collective-permute-start(bf16[256,512]{1,0:T(8,128)(2,1)S(1)} %collective-permute-done.11.refs_5_), channel_id=1, source_target_pairs={{0,8},{8,0},{16,24},{24,16},{1,9},{9,1},{17,25},{25,17},{2,10},{10... | collective-permute-start | bytes 786440 | tf_op jit(solution)/shard_map/ppermute | solution.py:298
  32.5 3.7 %collective-permute-start.20 = (f32[24,128]{1,0:T(8,128)S(1)}, f32[24,128]{1,0:T(8,128)S(1)}, u32[]{:S(2)}, u32[]{:S(2)}) collective-permute-start(f32[24,128]{1,0:T(8,128)S(1)} %add_add_fusion), channel_id=1, source_target_pairs={{0,16},{1,17},{2,18},{3,19},{4,20},{5,21},{6,22},{7,23},{8,24},{9,... | collective-permute-start | bytes 36872 | tf_op jit(solution)/shard_map/ppermute | solution.py:305
  36.2 1.2 %collective-permute-start.21 = (f32[24,128]{1,0:T(8,128)S(1)}, f32[24,128]{1,0:T(8,128)S(1)}, u32[]{:S(2)}, u32[]{:S(2)}) collective-permute-start(f32[24,128]{1,0:T(8,128)S(1)} %add.19.refs_0_), channel_id=1, source_target_pairs={{0,8},{8,0},{16,24},{24,16},{1,9},{9,1},{17,25},{25,17},{2,10},{10... | collective-permute-start | bytes 36872 | tf_op jit(solution)/shard_map/ppermute | solution.py:298

commit v2 on v0

--- a/solution.py
+++ b/solution.py
@@ -434,24 +434,23 @@
     dp_bits = [bit for bit in bits if bit < batches]
     core_bits = [bit for bit in bits if batches <= bit < batches * cores]
     y_bits = [bit for bit in bits if bit >= batches * cores]
-    share = step_sum(share, dp_bits[:1], devices, dkey_pre)
+    share = step_sum(share, core_bits + dp_bits[:1], devices, dkey_pre)
 
     q_grad, key_grad = call(
         functools.partial(grad_kernel, kv_heads, gsize),
         [shape((rows, width_q), bf), shape((rows, width_kv), bf)],
         [VMEM] * 3,
-    )(after(dscores, share), all_keys, queries)
+    )(after(dscores, (share, dvals_across)), all_keys, queries)
 
     for i in range(1, len(dp_bits), 2):
         share = step_sum(share, dp_bits[i : i + 2], devices, key_grad)
-    dvals_across = after(dvals_across, share)
     prefix_value_grad = summed(dval_pre, *dvals_across, *dvals_core, *to_core(dvals_across))
     dkeys_across = after(dkeys_across, (share, key_grad))
     prefix_key_grad = summed(dkey_pre, *dkeys_across, *dkeys_core, *to_core(dkeys_across))
 
     for bit in y_bits[1:]:
         share = step_sum(share, [bit], devices, prefix_value_grad)
-    shares = after(step_terms(share, core_bits + y_bits[:1], devices), (prefix_value_grad, prefix_key_grad))
+    shares = after(step_terms(share, y_bits[:1], devices), (prefix_value_grad, prefix_key_grad))
     q_total, v_total = call(
         functools.partial(last_kernel, devices),
         [shape((kv_heads * gsize, HEAD_DIM), f32), shape((kv_heads, HEAD_DIM), f32)],

time: 38.5 us -> 38.3 us (level)
  waiting for transfers between devices: 4.85 us -> 4.37 us
    ppermute x7, waiting for transfers between devices: 3.56 us -> 3.08 us  [step_terms(): lax.ppermute(x, ('resp', 'dp'), [(i, i ^ flip) for i in range(count)])]
    ppermute x16, starting transfers between devices: 10.6 us -> 11.1 us  [shifted(): return lax.ppermute(x, axis, pairs)]
where the time goes in v2:
time: 38.3 us; the launch traced here: 38.1 us
  starting transfers between devices  18.8 us (49%)
  Pallas kernels  12.1 us (32%)
  waiting for transfers between devices  4.37 us (11%)
  between operations  2.7 us (7%)
    ppermute x16, starting transfers between devices, shifted(): return lax.ppermute(x, axis, pairs)  11.1 us
    ppermute x7, starting transfers between devices, step_terms(): lax.ppermute(x, ('resp', 'dp'), [(i, i ^ flip) for i in range(count)])  7.76 us
    ppermute x7, waiting for transfers between devices, step_terms(): lax.ppermute(x, ('resp', 'dp'), [(i, i ^ flip) for i in range(count)])  3.08 us
    pallas_call x1, Pallas kernels, per_device(): call(functools.partial(self_kernel, kv_heads, gsize), [shape((kv_heads, g...  2.67 us
    pallas_call x1, Pallas kernels, per_device(): call(functools.partial(prob_kernel, kv_heads, gsize, count, len(keys_near...  2.57 us
    pallas_call x1, Pallas kernels, per_device(): call(functools.partial(score_kernel, kv_heads, gsize, count), [shape((kv_...  2.17 us
    pallas_call x2, Pallas kernels, summed(): call(functools.partial(sum_kernel, count), [shape((prefix_len, width_kv),...  1.83 us
    pallas_call x1, Pallas kernels, per_device(): call(functools.partial(grad_kernel, kv_heads, gsize), [shape((rows, width...  1.71 us
  transfers between devices with their start and end apart: 23, of which 6 were waited for; matrix products, arithmetic and copies ran while one was open for 0% of the time, Pallas kernels for 30%

profile of v2, /device:TPU:0, one launch (start us, length us, event | category | flops | bytes accessed | tf_op | source)
XLA Modules:
  0.0 38.1 jit_solution(9019526093847676183)
XLA Ops:
  0.6 0.0 copy-start.2
  0.7 0.0 copy-start
  0.7 3.0 %collective-permute-start.4 = (bf16[256,512]{1,0:T(8,128)(2,1)}, bf16[256,512]{1,0:T(8,128)(2,1)S(1)}, u32[]{:S(2)}, u32[]{:S(2)}) collective-permute-start(bf16[256,512]{1,0:T(8,128)(2,1)} %bitcast.18), channel_id=1, source_target_pairs={{0,16},{8,24},{16,0},{24,8},{1,17},{9,25},{17,1},{25,9},{2,18},{10... | collective-permute-start | bytes 786440 | tf_op jit(solution)/shard_map/ppermute | solution.py:298
  5.7 0.1 shard_map.162.info_ref.refs_0_
  5.7 0.5 %collective-permute-start.1 = (s32[8,128]{1,0:T(8,128)S(1)}, s32[8,128]{1,0:T(8,128)S(1)}, u32[]{:S(2)}, u32[]{:S(2)}) collective-permute-start(s32[8,128]{1,0:T(8,128)S(1)} %shard_map.162.info_ref.refs_0_), channel_id=1, source_target_pairs={{0,8},{8,0},{16,24},{24,16},{1,9},{9,1},{17,25},{25,17},{2,10},{10... | collective-permute-start | bytes 12296 | tf_op jit(solution)/shard_map/ppermute | solution.py:298
  6.2 0.1 collective-permute-start
  6.3 1.9 %collective-permute-start.3 = (bf16[256,512]{1,0:T(8,128)(2,1)}, bf16[256,512]{1,0:T(8,128)(2,1)S(1)}, u32[]{:S(2)}, u32[]{:S(2)}) collective-permute-start(bf16[256,512]{1,0:T(8,128)(2,1)} %bitcast.21), channel_id=1, source_target_pairs={{0,16},{8,24},{16,0},{24,8},{1,17},{9,25},{17,1},{25,9},{2,18},{10... | collective-permute-start | bytes 786440 | tf_op jit(solution)/shard_map/ppermute | solution.py:298
  8.3 2.7 %shard_map.163 = (bf16[4,640,128]{2,1,0:T(8,128)(2,1)S(1)}, bf16[4,640,128]{2,1,0:T(8,128)(2,1)S(1)}, f32[4,128,640]{2,1,0:T(8,128)S(1)}, f32[4,128,640]{2,1,0:T(8,128)S(1)}) custom-call(s32[8,128]{1,0:T(8,128)S(1)} %shard_map.162.info_ref.refs_0_, bf16[20,128]{1,0:T(8,128)(2,1)} %bitcast.30, bf16[128,512]{1,0:T(8,128)(2,1)} %bitcast.16, ...), custom_call_target="tpu_custom_call" | custom-call | flops 1000 | bytes 1000 | tf_op jit(solution)/shard_map/pallas_call | solution.py:366
  10.9 0.0 collective-permute-done.1.refs_2_
  11.0 0.2 collective-permute-done.refs_1_
  11.1 0.0 collective-permute-done.4.refs_5_
  11.1 0.0 collective-permute-done.5.refs_6_
  11.2 0.1 collective-permute-start.7
  11.3 0.5 %collective-permute-start.6 = (bf16[128,512]{1,0:T(8,128)(2,1)S(1)}, bf16[128,512]{1,0:T(8,128)(2,1)S(1)}, u32[]{:S(2)}, u32[]{:S(2)}) collective-permute-start(bf16[128,512]{1,0:T(8,128)(2,1)S(1)} %get-tuple-element.72), channel_id=1, source_target_pairs={{0,8},{8,0},{16,24},{24,16},{1,9},{9,1},{17,25},{25,17},{2,10},{10... | collective-permute-start | bytes 393224 | tf_op jit(solution)/shard_map/ppermute | solution.py:298
  11.7 0.1 collective-permute-start.2
  11.8 0.4 %collective-permute-start.8 = (bf16[256,512]{1,0:T(8,128)(2,1)S(1)}, bf16[256,512]{1,0:T(8,128)(2,1)S(1)}, u32[]{:S(2)}, u32[]{:S(2)}) collective-permute-start(bf16[256,512]{1,0:T(8,128)(2,1)S(1)} %bitcast.22), channel_id=1, source_target_pairs={{0,8},{8,0},{16,24},{24,16},{1,9},{9,1},{17,25},{25,17},{2,10},{10... | collective-permute-start | bytes 786440 | tf_op jit(solution)/shard_map/ppermute | solution.py:298
  12.3 0.7 %collective-permute-done.2.refs_3_ = s32[8,128]{1,0:T(8,128)S(1)} collective-permute-done((s32[8,128]{1,0:T(8,128)S(1)}, s32[8,128]{1,0:T(8,128)S(1)}, u32[]{:S(2)}, u32[]{:S(2)}) %collective-permute-start.2) | collective-permute-done | bytes 4128 | tf_op jit(solution)/shard_map/ppermute | solution.py:298
  12.9 0.0 collective-permute-done.7.refs_8_
  12.9 2.6 %shard_map.164 = (bf16[384,512]{1,0:T(8,128)(2,1)S(1)}, bf16[4,384,640]{2,1,0:T(8,128)(2,1)S(1)}, bf16[256,512]{1,0:T(8,128)(2,1)S(1)}, bf16[128,512]{1,0:T(8,128)(2,1)}, f32[4,128]{1,0:T(4,128)S(1)}) custom-call(s32[8,128]{1,0:T(8,128)S(1)} %shard_map.162.info_ref.refs_0_, s32[8,128]{1,0:T(8,128)S(1)} %collective-permute-done.refs_1_, ...), custom_call_target="tpu_custom_call" | custom-call | flops 1000 | bytes 1000 | tf_op jit(solution)/shard_map/pallas_call | solution.py:397
  15.5 0.4 %collective-permute-done.3.refs_5_ = bf16[256,512]{1,0:T(8,128)(2,1)S(1)} collective-permute-done((bf16[256,512]{1,0:T(8,128)(2,1)}, bf16[256,512]{1,0:T(8,128)(2,1)S(1)}, u32[]{:S(2)}, u32[]{:S(2)}) %collective-permute-start.3) | collective-permute-done | bytes 262176 | tf_op jit(solution)/shard_map/ppermute | solution.py:298
  15.9 1.8 %collective-permute-start.13 = (bf16[256,512]{1,0:T(8,128)(2,1)S(1)}, bf16[256,512]{1,0:T(8,128)(2,1)S(1)}, u32[]{:S(2)}, u32[]{:S(2)}) collective-permute-start(bf16[256,512]{1,0:T(8,128)(2,1)S(1)} %get-tuple-element.66.refs_4_), channel_id=1, source_target_pairs={{0,16},{8,24},{16,0},{24,8},{1,17},{9,25},{17,1},{25,9},{2,18},{10... | collective-permute-start | bytes 786440 | tf_op jit(solution)/shard_map/ppermute | solution.py:298
  17.8 0.0 collective-permute-done.8.refs_6_
  17.8 0.0 collective-permute-done.9.refs_7_
  17.8 2.2 %shard_map.165 = (bf16[4,384,640]{2,1,0:T(8,128)(2,1)S(1)}, f32[24,128]{1,0:T(8,128)S(1)}) custom-call(s32[8,128]{1,0:T(8,128)S(1)} %shard_map.162.info_ref.refs_0_, s32[8,128]{1,0:T(8,128)S(1)} %collective-permute-done.refs_1_, s32[8,128]{1,0:T(8,128)S(1)} %collective-permute-done.1.refs_2_, s32[8,128]{1,0:T(8,128)S(1)} %collective-permute-done.2.refs_3_, ...), custom_call_target="tpu_custom_call" | custom-call | flops 1000 | bytes 1000 | tf_op jit(solution)/shard_map/pallas_call | solution.py:413
  19.9 1.3 %collective-permute-start.12 = (f32[24,128]{1,0:T(8,128)S(1)}, f32[24,128]{1,0:T(8,128)S(1)}, u32[]{:S(2)}, u32[]{:S(2)}) collective-permute-start(f32[24,128]{1,0:T(8,128)S(1)} %get-tuple-element.52), channel_id=1, source_target_pairs={{0,9},{1,8},{2,11},{3,10},{4,13},{5,12},{6,15},{7,14},{8,1},{9,0},... | collective-permute-start | bytes 36872 | tf_op jit(solution)/shard_map/ppermute | solution.py:305
  21.2 0.5 %collective-permute-start.11 = (f32[24,128]{1,0:T(8,128)S(1)}, f32[24,128]{1,0:T(8,128)S(1)}, u32[]{:S(2)}, u32[]{:S(2)}) collective-permute-start(f32[24,128]{1,0:T(8,128)S(1)} %get-tuple-element.52), channel_id=1, source_target_pairs={{0,1},{1,0},{2,3},{3,2},{4,5},{5,4},{6,7},{7,6},{8,9},{9,8},{10,11... | collective-permute-start | bytes 36872 | tf_op jit(solution)/shard_map/ppermute | solution.py:305
  21.7 0.1 collective-permute-start.10
  21.8 0.5 %shard_map.166.refs_4_ = bf16[256,512]{1,0:T(8,128)(2,1)S(1)} custom-call(bf16[4,384,640]{2,1,0:T(8,128)(2,1)S(1)} %get-tuple-element.57.ds_ref, bf16[4,640,128]{2,1,0:T(8,128)(2,1)S(1)} %get-tuple-element.43.refs_10_.qs_ref), custom_call_target="tpu_custom_call" | custom-call | flops 1000 | bytes 1000 | tf_op jit(solution)/shard_map/pallas_call | solution.py:425
  22.3 1.5 %collective-permute-start.14 = (bf16[256,512]{1,0:T(8,128)(2,1)S(1)}, bf16[256,512]{1,0:T(8,128)(2,1)S(1)}, u32[]{:S(2)}, u32[]{:S(2)}) collective-permute-start(bf16[256,512]{1,0:T(8,128)(2,1)S(1)} %shard_map.166.refs_4_), channel_id=1, source_target_pairs={{0,16},{8,24},{16,0},{24,8},{1,17},{9,25},{17,1},{25,9},{2,18},{10... | collective-permute-start | bytes 786440 | tf_op jit(solution)/shard_map/ppermute | solution.py:298
  23.8 0.0 collective-permute-done.12
  23.8 1.1 %collective-permute-done.11 = f32[24,128]{1,0:T(8,128)S(1)} collective-permute-done((f32[24,128]{1,0:T(8,128)S(1)}, f32[24,128]{1,0:T(8,128)S(1)}, u32[]{:S(2)}, u32[]{:S(2)}) %collective-permute-start.11) | collective-permute-done | bytes 12320 | tf_op jit(solution)/shard_map/ppermute | solution.py:305
  24.9 3.7 %collective-permute-start.17 = (f32[24,128]{1,0:T(8,128)S(1)}, f32[24,128]{1,0:T(8,128)S(1)}, u32[]{:S(2)}, u32[]{:S(2)}) collective-permute-start(f32[24,128]{1,0:T(8,128)S(1)} %add_add_fusion.1), channel_id=1, source_target_pairs={{0,6},{1,7},{2,4},{3,5},{4,2},{5,3},{6,0},{7,1},{8,14},{9,15},{10,... | collective-permute-start | bytes 36872 | tf_op jit(solution)/shard_map/ppermute | solution.py:305
  28.6 0.0 collective-permute-start.16
  28.6 0.8 %collective-permute-start.15 = (f32[24,128]{1,0:T(8,128)S(1)}, f32[24,128]{1,0:T(8,128)S(1)}, u32[]{:S(2)}, u32[]{:S(2)}) collective-permute-start(f32[24,128]{1,0:T(8,128)S(1)} %add_add_fusion.1), channel_id=1, source_target_pairs={{0,2},{1,3},{2,0},{3,1},{4,6},{5,7},{6,4},{7,5},{8,10},{9,11},{10,... | collective-permute-start | bytes 36872 | tf_op jit(solution)/shard_map/ppermute | solution.py:305
  29.4 0.0 collective-permute-done.13.refs_5_
  29.4 0.0 collective-permute-start.18
  29.4 1.7 %shard_map.167 = (bf16[128,2560]{1,0:T(8,128)(2,1)}, bf16[128,512]{1,0:T(8,128)(2,1)}) custom-call(bf16[4,384,640]{2,1,0:T(8,128)(2,1)S(1)} %get-tuple-element.57.ds_ref, bf16[384,512]{1,0:T(8,128)(2,1)S(1)} %get-tuple-element.49.refs_11_.ka_ref, bf16[4,640,128]{2,1,0:T(8,128)(2,1)S(1)} %get-tuple-element.43.refs_10_.qs_ref), custom_call_target="tpu_custom_call" | custom-call | flops 1000 | bytes 1000 | tf_op jit(solution)/shard_map/pallas_call | solution.py:439
  31.1 0.0 collective-permute-done.17
  31.1 0.5 %collective-permute-start.20 = (bf16[256,512]{1,0:T(8,128)(2,1)S(1)}, bf16[256,512]{1,0:T(8,128)(2,1)S(1)}, u32[]{:S(2)}, u32[]{:S(2)}) collective-permute-start(bf16[256,512]{1,0:T(8,128)(2,1)S(1)} %get-tuple-element.66.refs_4_), channel_id=1, source_target_pairs={{0,8},{8,0},{16,24},{24,16},{1,9},{9,1},{17,25},{25,17},{2,10},{10... | collective-permute-start | bytes 786440 | tf_op jit(solution)/shard_map/ppermute | solution.py:298
  31.6 1.6 %collective-permute-done.16 = f32[24,128]{1,0:T(8,128)S(1)} collective-permute-done((f32[24,128]{1,0:T(8,128)S(1)}, f32[24,128]{1,0:T(8,128)S(1)}, u32[]{:S(2)}, u32[]{:S(2)}) %collective-permute-start.16) | collective-permute-done | bytes 12320 | tf_op jit(solution)/shard_map/ppermute | solution.py:305
  33.2 0.0 collective-permute-start.21
  33.2 0.0 collective-permute-done.15
  33.2 0.6 %collective-permute-start.19 = (bf16[256,512]{1,0:T(8,128)(2,1)S(1)}, bf16[256,512]{1,0:T(8,128)(2,1)S(1)}, u32[]{:S(2)}, u32[]{:S(2)}) collective-permute-start(bf16[256,512]{1,0:T(8,128)(2,1)S(1)} %collective-permute-done.14.refs_5_), channel_id=1, source_target_pairs={{0,8},{8,0},{16,24},{24,16},{1,9},{9,1},{17,25},{25,17},{2,10},{10... | collective-permute-start | bytes 786440 | tf_op jit(solution)/shard_map/ppermute | solution.py:298
  33.8 1.4 %collective-permute-start.22 = (f32[24,128]{1,0:T(8,128)S(1)}, f32[24,128]{1,0:T(8,128)S(1)}, u32[]{:S(2)}, u32[]{:S(2)}) collective-permute-start(f32[24,128]{1,0:T(8,128)S(1)} %add_add_fusion.refs_0_), channel_id=1, source_target_pairs={{0,16},{1,17},{2,18},{3,19},{4,20},{5,21},{6,22},{7,23},{8,24},{9,... | collective-permute-start | bytes 36872 | tf_op jit(solution)/shard_map/ppermute | solution.py:305
  35.2 0.9 %shard_map.169 = bf16[256,512]{1,0:T(8,128)(2,1)} custom-call(s32[8,128]{1,0:T(8,128)S(1)} %shard_map.162.info_ref.refs_0_, s32[8,128]{1,0:T(8,128)S(1)} %collective-permute-done.refs_1_, s32[8,128]{1,0:T(8,128)S(1)} %collective-permute-done.1.refs_2_, s32[8,128]{1,0:T(8,128)S(1)} %collective-permute-done.2.refs_3_, ...), custom_call_target="tpu_custom_call" | custom-call | flops 1000 | bytes 1000 | tf_op jit(solution)/shard_map/pallas_call | solution.py:346
  36.1 0.9 %shard_map.168 = bf16[256,512]{1,0:T(8,128)(2,1)} custom-call(s32[8,128]{1,0:T(8,128)S(1)} %shard_map.162.info_ref.refs_0_, s32[8,128]{1,0:T(8,128)S(1)} %collective-permute-done.refs_1_, s32[8,128]{1,0:T(8,128)S(1)} %collective-permute-done.1.refs_2_, s32[8,128]{1,0:T(8,128)S(1)} %collective-permute-done.2.refs_3_, ...), custom_call_target="tpu_custom_call" | custom-call | flops 1000 | bytes 1000 | tf_op jit(solution)/shard_map/pallas_call | solution.py:346
  37.1 0.4 %collective-permute-done.22.refs_1_ = f32[24,128]{1,0:T(8,128)S(1)} collective-permute-done((f32[24,128]{1,0:T(8,128)S(1)}, f32[24,128]{1,0:T(8,128)S(1)}, u32[]{:S(2)}, u32[]{:S(2)}) %collective-permute-start.22) | collective-permute-done | bytes 12320 | tf_op jit(solution)/shard_map/ppermute | solution.py:305
  37.5 0.6 %shard_map.170 = (f32[20,128]{1,0:T(8,128)}, f32[4,128]{1,0:T(4,128)}) custom-call(f32[24,128]{1,0:T(8,128)S(1)} %add_add_fusion.refs_0_, f32[24,128]{1,0:T(8,128)S(1)} %collective-permute-done.22.refs_1_), custom_call_target="tpu_custom_call" | custom-call | flops 1000 | bytes 1000 | tf_op jit(solution)/shard_map/pallas_call | solution.py:454
  (18 shorter events, 0.1 us)
Async XLA Ops:
  0.6 12.3 %copy-start.1 = (bf16[1,1,256,512]{3,2,1,0:T(8,128)(2,1)S(1)}, bf16[1,1,256,512]{3,2,1,0:T(8,128)(2,1)}, u32[]{:S(2)}) copy-start(bf16[1,1,256,512]{3,2,1,0:T(8,128)(2,1)} %param.14) | copy-start | bytes 786436
  0.6 11.2 %copy-start.2 = (bf16[1,1,256,512]{3,2,1,0:T(8,128)(2,1)S(1)}, bf16[1,1,256,512]{3,2,1,0:T(8,128)(2,1)}, u32[]{:S(2)}) copy-start(bf16[1,1,256,512]{3,2,1,0:T(8,128)(2,1)} %param.15) | copy-start | bytes 786436
  0.7 12.3 %copy-start = (bf16[1,1,128,512]{3,2,1,0:T(8,128)(2,1)S(1)}, bf16[1,1,128,512]{3,2,1,0:T(8,128)(2,1)}, u32[]{:S(2)}) copy-start(bf16[1,1,128,512]{3,2,1,0:T(8,128)(2,1)} %param.12) | copy-start | bytes 393220
  0.7 12.3 %copy-start.3 = (s32[1,1,2]{2,1,0:T(1,128)S(1)}, s32[1,1,2]{2,1,0:T(1,128)}, u32[]{:S(2)}) copy-start(s32[1,1,2]{2,1,0:T(1,128)} %param.21) | copy-start | bytes 28
  0.7 10.5 %collective-permute-start.4 = (bf16[256,512]{1,0:T(8,128)(2,1)}, bf16[256,512]{1,0:T(8,128)(2,1)S(1)}, u32[]{:S(2)}, u32[]{:S(2)}) collective-permute-start(bf16[256,512]{1,0:T(8,128)(2,1)} %bitcast.18), channel_id=1, source_target_pairs={{0,16},{8,24},{16,0},{24,8},{1,17},{9,25},{17,1},{25,9},{2,18},{10... | collective-permute-start | bytes 786440 | tf_op jit(solution)/shard_map/ppermute | solution.py:298
  3.7 7.4 %collective-permute-start.5 = (bf16[256,512]{1,0:T(8,128)(2,1)}, bf16[256,512]{1,0:T(8,128)(2,1)S(1)}, u32[]{:S(2)}, u32[]{:S(2)}) collective-permute-start(bf16[256,512]{1,0:T(8,128)(2,1)} %bitcast.19), channel_id=1, source_target_pairs={{0,8},{8,0},{16,24},{24,16},{1,9},{9,1},{17,25},{25,17},{2,10},{10... | collective-permute-start | bytes 786440 | tf_op jit(solution)/shard_map/ppermute | solution.py:298
  5.7 5.2 %collective-permute-start.1 = (s32[8,128]{1,0:T(8,128)S(1)}, s32[8,128]{1,0:T(8,128)S(1)}, u32[]{:S(2)}, u32[]{:S(2)}) collective-permute-start(s32[8,128]{1,0:T(8,128)S(1)} %shard_map.162.info_ref.refs_0_), channel_id=1, source_target_pairs={{0,8},{8,0},{16,24},{24,16},{1,9},{9,1},{17,25},{25,17},{2,10},{10... | collective-permute-start | bytes 12296 | tf_op jit(solution)/shard_map/ppermute | solution.py:298
  6.2 4.9 %collective-permute-start = (s32[8,128]{1,0:T(8,128)S(1)}, s32[8,128]{1,0:T(8,128)S(1)}, u32[]{:S(2)}, u32[]{:S(2)}) collective-permute-start(s32[8,128]{1,0:T(8,128)S(1)} %shard_map.162.info_ref.refs_0_), channel_id=1, source_target_pairs={{0,16},{8,24},{16,0},{24,8},{1,17},{9,25},{17,1},{25,9},{2,18},{10... | collective-permute-start | bytes 12296 | tf_op jit(solution)/shard_map/ppermute | solution.py:298
  6.3 9.6 %collective-permute-start.3 = (bf16[256,512]{1,0:T(8,128)(2,1)}, bf16[256,512]{1,0:T(8,128)(2,1)S(1)}, u32[]{:S(2)}, u32[]{:S(2)}) collective-permute-start(bf16[256,512]{1,0:T(8,128)(2,1)} %bitcast.21), channel_id=1, source_target_pairs={{0,16},{8,24},{16,0},{24,8},{1,17},{9,25},{17,1},{25,9},{2,18},{10... | collective-permute-start | bytes 786440 | tf_op jit(solution)/shard_map/ppermute | solution.py:298
  11.2 1.7 %collective-permute-start.7 = (bf16[128,512]{1,0:T(8,128)(2,1)S(1)}, bf16[128,512]{1,0:T(8,128)(2,1)S(1)}, u32[]{:S(2)}, u32[]{:S(2)}) collective-permute-start(bf16[128,512]{1,0:T(8,128)(2,1)S(1)} %get-tuple-element.71), channel_id=1, source_target_pairs={{0,8},{8,0},{16,24},{24,16},{1,9},{9,1},{17,25},{25,17},{2,10},{10... | collective-permute-start | bytes 393224 | tf_op jit(solution)/shard_map/ppermute | solution.py:298
  11.3 1.7 %collective-permute-start.6 = (bf16[128,512]{1,0:T(8,128)(2,1)S(1)}, bf16[128,512]{1,0:T(8,128)(2,1)S(1)}, u32[]{:S(2)}, u32[]{:S(2)}) collective-permute-start(bf16[128,512]{1,0:T(8,128)(2,1)S(1)} %get-tuple-element.72), channel_id=1, source_target_pairs={{0,8},{8,0},{16,24},{24,16},{1,9},{9,1},{17,25},{25,17},{2,10},{10... | collective-permute-start | bytes 393224 | tf_op jit(solution)/shard_map/ppermute | solution.py:298
  11.7 1.2 %collective-permute-start.2 = (s32[8,128]{1,0:T(8,128)S(1)}, s32[8,128]{1,0:T(8,128)S(1)}, u32[]{:S(2)}, u32[]{:S(2)}) collective-permute-start(s32[8,128]{1,0:T(8,128)S(1)} %collective-permute-done.refs_1_), channel_id=1, source_target_pairs={{0,8},{8,0},{16,24},{24,16},{1,9},{9,1},{17,25},{25,17},{2,10},{10... | collective-permute-start | bytes 12296 | tf_op jit(solution)/shard_map/ppermute | solution.py:298
  11.8 5.9 %collective-permute-start.8 = (bf16[256,512]{1,0:T(8,128)(2,1)S(1)}, bf16[256,512]{1,0:T(8,128)(2,1)S(1)}, u32[]{:S(2)}, u32[]{:S(2)}) collective-permute-start(bf16[256,512]{1,0:T(8,128)(2,1)S(1)} %bitcast.22), channel_id=1, source_target_pairs={{0,8},{8,0},{16,24},{24,16},{1,9},{9,1},{17,25},{25,17},{2,10},{10... | collective-permute-start | bytes 786440 | tf_op jit(solution)/shard_map/ppermute | solution.py:298
  15.9 1.8 %collective-permute-start.9 = (bf16[256,512]{1,0:T(8,128)(2,1)S(1)}, bf16[256,512]{1,0:T(8,128)(2,1)S(1)}, u32[]{:S(2)}, u32[]{:S(2)}) collective-permute-start(bf16[256,512]{1,0:T(8,128)(2,1)S(1)} %collective-permute-done.3.refs_5_), channel_id=1, source_target_pairs={{0,8},{8,0},{16,24},{24,16},{1,9},{9,1},{17,25},{25,17},{2,10},{10... | collective-permute-start | bytes 786440 | tf_op jit(solution)/shard_map/ppermute | solution.py:298
  15.9 13.4 %collective-permute-start.13 = (bf16[256,512]{1,0:T(8,128)(2,1)S(1)}, bf16[256,512]{1,0:T(8,128)(2,1)S(1)}, u32[]{:S(2)}, u32[]{:S(2)}) collective-permute-start(bf16[256,512]{1,0:T(8,128)(2,1)S(1)} %get-tuple-element.66.refs_4_), channel_id=1, source_target_pairs={{0,16},{8,24},{16,0},{24,8},{1,17},{9,25},{17,1},{25,9},{2,18},{10... | collective-permute-start | bytes 786440 | tf_op jit(solution)/shard_map/ppermute | solution.py:298
  19.9 3.9 %collective-permute-start.12 = (f32[24,128]{1,0:T(8,128)S(1)}, f32[24,128]{1,0:T(8,128)S(1)}, u32[]{:S(2)}, u32[]{:S(2)}) collective-permute-start(f32[24,128]{1,0:T(8,128)S(1)} %get-tuple-element.52), channel_id=1, source_target_pairs={{0,9},{1,8},{2,11},{3,10},{4,13},{5,12},{6,15},{7,14},{8,1},{9,0},... | collective-permute-start | bytes 36872 | tf_op jit(solution)/shard_map/ppermute | solution.py:305
  21.2 3.7 %collective-permute-start.11 = (f32[24,128]{1,0:T(8,128)S(1)}, f32[24,128]{1,0:T(8,128)S(1)}, u32[]{:S(2)}, u32[]{:S(2)}) collective-permute-start(f32[24,128]{1,0:T(8,128)S(1)} %get-tuple-element.52), channel_id=1, source_target_pairs={{0,1},{1,0},{2,3},{3,2},{4,5},{5,4},{6,7},{7,6},{8,9},{9,8},{10,11... | collective-permute-start | bytes 36872 | tf_op jit(solution)/shard_map/ppermute | solution.py:305
  21.7 3.2 %collective-permute-start.10 = (f32[24,128]{1,0:T(8,128)S(1)}, f32[24,128]{1,0:T(8,128)S(1)}, u32[]{:S(2)}, u32[]{:S(2)}) collective-permute-start(f32[24,128]{1,0:T(8,128)S(1)} %get-tuple-element.52), channel_id=1, source_target_pairs={{0,8},{1,9},{2,10},{3,11},{4,12},{5,13},{6,14},{7,15},{8,0},{9,1},... | collective-permute-start | bytes 36872 | tf_op jit(solution)/shard_map/ppermute | solution.py:305
  22.3 10.9 %collective-permute-start.14 = (bf16[256,512]{1,0:T(8,128)(2,1)S(1)}, bf16[256,512]{1,0:T(8,128)(2,1)S(1)}, u32[]{:S(2)}, u32[]{:S(2)}) collective-permute-start(bf16[256,512]{1,0:T(8,128)(2,1)S(1)} %shard_map.166.refs_4_), channel_id=1, source_target_pairs={{0,16},{8,24},{16,0},{24,8},{1,17},{9,25},{17,1},{25,9},{2,18},{10... | collective-permute-start | bytes 786440 | tf_op jit(solution)/shard_map/ppermute | solution.py:298
  24.9 6.2 %collective-permute-start.17 = (f32[24,128]{1,0:T(8,128)S(1)}, f32[24,128]{1,0:T(8,128)S(1)}, u32[]{:S(2)}, u32[]{:S(2)}) collective-permute-start(f32[24,128]{1,0:T(8,128)S(1)} %add_add_fusion.1), channel_id=1, source_target_pairs={{0,6},{1,7},{2,4},{3,5},{4,2},{5,3},{6,0},{7,1},{8,14},{9,15},{10,... | collective-permute-start | bytes 36872 | tf_op jit(solution)/shard_map/ppermute | solution.py:305
  28.6 4.6 %collective-permute-start.16 = (f32[24,128]{1,0:T(8,128)S(1)}, f32[24,128]{1,0:T(8,128)S(1)}, u32[]{:S(2)}, u32[]{:S(2)}) collective-permute-start(f32[24,128]{1,0:T(8,128)S(1)} %add_add_fusion.1), channel_id=1, source_target_pairs={{0,4},{1,5},{2,6},{3,7},{4,0},{5,1},{6,2},{7,3},{8,12},{9,13},{10,... | collective-permute-start | bytes 36872 | tf_op jit(solution)/shard_map/ppermute | solution.py:305
  28.6 4.6 %collective-permute-start.15 = (f32[24,128]{1,0:T(8,128)S(1)}, f32[24,128]{1,0:T(8,128)S(1)}, u32[]{:S(2)}, u32[]{:S(2)}) collective-permute-start(f32[24,128]{1,0:T(8,128)S(1)} %add_add_fusion.1), channel_id=1, source_target_pairs={{0,2},{1,3},{2,0},{3,1},{4,6},{5,7},{6,4},{7,5},{8,10},{9,11},{10,... | collective-permute-start | bytes 36872 | tf_op jit(solution)/shard_map/ppermute | solution.py:305
  29.4 6.7 %collective-permute-start.18 = (bf16[256,512]{1,0:T(8,128)(2,1)S(1)}, bf16[256,512]{1,0:T(8,128)(2,1)S(1)}, u32[]{:S(2)}, u32[]{:S(2)}) collective-permute-start(bf16[256,512]{1,0:T(8,128)(2,1)S(1)} %shard_map.166.refs_4_), channel_id=1, source_target_pairs={{0,8},{8,0},{16,24},{24,16},{1,9},{9,1},{17,25},{25,17},{2,10},{10... | collective-permute-start | bytes 786440 | tf_op jit(solution)/shard_map/ppermute | solution.py:298
  31.1 4.1 %collective-permute-start.20 = (bf16[256,512]{1,0:T(8,128)(2,1)S(1)}, bf16[256,512]{1,0:T(8,128)(2,1)S(1)}, u32[]{:S(2)}, u32[]{:S(2)}) collective-permute-start(bf16[256,512]{1,0:T(8,128)(2,1)S(1)} %get-tuple-element.66.refs_4_), channel_id=1, source_target_pairs={{0,8},{8,0},{16,24},{24,16},{1,9},{9,1},{17,25},{25,17},{2,10},{10... | collective-permute-start | bytes 786440 | tf_op jit(solution)/shard_map/ppermute | solution.py:298
  33.2 2.0 %collective-permute-start.21 = (bf16[256,512]{1,0:T(8,128)(2,1)S(1)}, bf16[256,512]{1,0:T(8,128)(2,1)S(1)}, u32[]{:S(2)}, u32[]{:S(2)}) collective-permute-start(bf16[256,512]{1,0:T(8,128)(2,1)S(1)} %collective-permute-done.13.refs_5_), channel_id=1, source_target_pairs={{0,8},{8,0},{16,24},{24,16},{1,9},{9,1},{17,25},{25,17},{2,10},{10... | collective-permute-start | bytes 786440 | tf_op jit(solution)/shard_map/ppermute | solution.py:298
  33.2 2.9 %collective-permute-start.19 = (bf16[256,512]{1,0:T(8,128)(2,1)S(1)}, bf16[256,512]{1,0:T(8,128)(2,1)S(1)}, u32[]{:S(2)}, u32[]{:S(2)}) collective-permute-start(bf16[256,512]{1,0:T(8,128)(2,1)S(1)} %collective-permute-done.14.refs_5_), channel_id=1, source_target_pairs={{0,8},{8,0},{16,24},{24,16},{1,9},{9,1},{17,25},{25,17},{2,10},{10... | collective-permute-start | bytes 786440 | tf_op jit(solution)/shard_map/ppermute | solution.py:298
  33.8 3.7 %collective-permute-start.22 = (f32[24,128]{1,0:T(8,128)S(1)}, f32[24,128]{1,0:T(8,128)S(1)}, u32[]{:S(2)}, u32[]{:S(2)}) collective-permute-start(f32[24,128]{1,0:T(8,128)S(1)} %add_add_fusion.refs_0_), channel_id=1, source_target_pairs={{0,16},{1,17},{2,18},{3,19},{4,20},{5,21},{6,22},{7,23},{8,24},{9,... | collective-permute-start | bytes 36872 | tf_op jit(solution)/shard_map/ppermute | solution.py:305

commit v3 on v1

--- a/solution.py
+++ b/solution.py
@@ -47,7 +47,7 @@
     kv_heads,
     gsize,
     info_ref,
-    bias_hbm,
+    bias_ref,
     k_hbm,
     v_hbm,
     q_hbm,
@@ -56,7 +56,6 @@
     gs_ref,
     ss_ref,
     dp_ref,
-    bias_ref,
     k_ref,
     v_ref,
     q_ref,
@@ -73,7 +72,6 @@
     for k in range(kv_heads):
         cols = heads(k, gsize)
         if not k:
-            fetch(bias_hbm, bias_ref)
             fetch(k_hbm, k_ref)
         fetch(q_hbm.at[:, cols], q_ref.at[:, cols])
         if not k:
@@ -84,10 +82,9 @@
     pos_t = lax.broadcasted_iota(jnp.int32, (rows, rows), 1)
     causal = pos_u <= pos_t
     live = lax.broadcasted_iota(jnp.int32, (rows, HEAD_DIM), 0) < info_ref[LENGTH : LENGTH + 1, :]
-    copies[0].wait()
     bias = bias_ref[...].astype(jnp.float32)
     for k in range(kv_heads):
-        for copy in copies[1:5] if not k else copies[3 + 2 * k : 5 + 2 * k]:
+        for copy in copies[:4] if not k else copies[2 + 2 * k : 4 + 2 * k]:
             copy.wait()
         keys = k_ref[:, head(k)]
         vals = v_ref[:, head(k)]
@@ -371,21 +368,18 @@
             shape((kv_heads, rows, gsize * rows), f32),
             shape((kv_heads, rows, gsize * rows), f32),
         ],
-        [VMEM] + [HBM] * 5,
+        [VMEM] * 2 + [HBM] * 4,
         scratch=[
-            pltpu.VMEM((kv_heads * gsize, HEAD_DIM), bf),
             pltpu.VMEM((rows, width_kv), bf),
             pltpu.VMEM((rows, width_kv), bf),
             pltpu.VMEM((rows, width_q), bf),
             pltpu.VMEM((rows, width_q), bf),
-            pltpu.SemaphoreType.DMA((3 + 2 * kv_heads,)),
+            pltpu.SemaphoreType.DMA((2 + 2 * kv_heads,)),
         ],
     )(
         info,
-        *map(
-            in_hbm,
-            (q_bias.reshape(-1, HEAD_DIM), key_in[0, 0], value_in[0, 0], query_in[0, 0], out_grad[0, 0]),
-        ),
+        q_bias.reshape(-1, HEAD_DIM),
+        *map(in_hbm, (key_in[0, 0], value_in[0, 0], query_in[0, 0], out_grad[0, 0])),
     )
     infos = spread(info)
     keys_across = after(keys_across, (infos[: chips + 1], d_self))

time: 38.2 us -> 38.2 us (level)
  local copies, waits for them, and re-layouts: 0.04 us -> 0.73 us
  waiting for transfers between devices: 5.17 us -> 4.58 us
    unnamed x8 -> x10, local copies, waits for them, and re-layouts: 0.02 us -> 0.71 us
    ppermute x17, waiting for transfers between devices: 1.53 us -> 0.94 us  [shifted(): return lax.ppermute(x, axis, pairs)]
  transfers between devices with their start and end apart: 22 -> 22, of which waited for: 7 -> 5; matrix products, arithmetic and copies ran while one was open for 0% -> 0% of each run, Pallas kernels for 30% -> 30%
where the time goes in v3:
time: 38.2 us; the launch traced here: 38 us
  starting transfers between devices  17.8 us (47%)
  Pallas kernels  12.1 us (32%)
  waiting for transfers between devices  4.58 us (12%)
  between operations  2.73 us (7%)
  local copies, waits for them, and re-layouts  0.73 us (2%)
    ppermute x17, starting transfers between devices, shifted(): return lax.ppermute(x, axis, pairs)  10.5 us
    ppermute x5, starting transfers between devices, step_terms(): lax.ppermute(x, ('resp', 'dp'), [(i, i ^ flip) for i in range(count)])  7.33 us
    ppermute x5, waiting for transfers between devices, step_terms(): lax.ppermute(x, ('resp', 'dp'), [(i, i ^ flip) for i in range(count)])  3.64 us
    pallas_call x1, Pallas kernels, per_device(): call(functools.partial(self_kernel, kv_heads, gsize), [shape((kv_heads, g...  2.66 us
    pallas_call x1, Pallas kernels, per_device(): call(functools.partial(prob_kernel, kv_heads, gsize, count, len(keys_near...  2.57 us
    pallas_call x1, Pallas kernels, per_device(): call(functools.partial(score_kernel, kv_heads, gsize, count), [shape((kv_...  2.17 us
    pallas_call x2, Pallas kernels, summed(): call(functools.partial(sum_kernel, count), [shape((prefix_len, width_kv),...  1.83 us
    pallas_call x1, Pallas kernels, per_device(): call(functools.partial(grad_kernel, kv_heads, gsize), [shape((rows, width...  1.71 us
  transfers between devices with their start and end apart: 22, of which 5 were waited for; matrix products, arithmetic and copies ran while one was open for 0% of the time, Pallas kernels for 30%

profile of v3, /device:TPU:0, one launch (start us, length us, event | category | flops | bytes accessed | tf_op | source)
XLA Modules:
  0.0 38.0 jit_solution(5736288772263869062)
XLA Ops:
  0.6 0.0 copy-start.2
  0.7 0.0 copy-start
  0.7 3.0 %collective-permute-start.4 = (bf16[256,512]{1,0:T(8,128)(2,1)}, bf16[256,512]{1,0:T(8,128)(2,1)S(1)}, u32[]{:S(2)}, u32[]{:S(2)}) collective-permute-start(bf16[256,512]{1,0:T(8,128)(2,1)} %bitcast.18), channel_id=1, source_target_pairs={{0,16},{8,24},{16,0},{24,8},{1,17},{9,25},{17,1},{25,9},{2,18},{10... | collective-permute-start | bytes 786440 | tf_op jit(solution)/shard_map/ppermute | solution.py:295
  3.7 0.0 collective-permute-start.5
  5.6 0.1 shard_map.162.info_ref.refs_0_
  5.7 0.5 %collective-permute-start.1 = (s32[8,128]{1,0:T(8,128)S(1)}, s32[8,128]{1,0:T(8,128)S(1)}, u32[]{:S(2)}, u32[]{:S(2)}) collective-permute-start(s32[8,128]{1,0:T(8,128)S(1)} %shard_map.162.info_ref.refs_0_), channel_id=1, source_target_pairs={{0,8},{8,0},{16,24},{24,16},{1,9},{9,1},{17,25},{25,17},{2,10},{10... | collective-permute-start | bytes 12296 | tf_op jit(solution)/shard_map/ppermute | solution.py:295
  6.2 0.1 collective-permute-start
  6.3 1.9 %collective-permute-start.3 = (bf16[256,512]{1,0:T(8,128)(2,1)}, bf16[256,512]{1,0:T(8,128)(2,1)S(1)}, u32[]{:S(2)}, u32[]{:S(2)}) collective-permute-start(bf16[256,512]{1,0:T(8,128)(2,1)} %bitcast.21), channel_id=1, source_target_pairs={{0,16},{8,24},{16,0},{24,8},{1,17},{9,25},{17,1},{25,9},{2,18},{10... | collective-permute-start | bytes 786440 | tf_op jit(solution)/shard_map/ppermute | solution.py:295
  8.3 0.7 %copy-done.3 = bf16[2560]{0:T(1024)(128)(2,1)S(1)} copy-done((bf16[2560]{0:T(1024)(128)(2,1)S(1)}, bf16[2560]{0:T(1024)(128)(2,1)}, u32[]{:S(2)}) %copy-start.3) | copy-done | bytes 5144
  9.0 2.7 %shard_map.163 = (bf16[4,640,128]{2,1,0:T(8,128)(2,1)S(1)}, bf16[4,640,128]{2,1,0:T(8,128)(2,1)S(1)}, f32[4,128,640]{2,1,0:T(8,128)S(1)}, f32[4,128,640]{2,1,0:T(8,128)S(1)}) custom-call(s32[8,128]{1,0:T(8,128)S(1)} %shard_map.162.info_ref.refs_0_, bf16[20,128]{1,0:T(8,128)(2,1)S(1)} %bitcast.24, bf16[128,512]{1,0:T(8,128)(2,1)} %bitcast.16, ...), custom_call_target="tpu_custom_call" | custom-call | flops 1000 | bytes 1000 | tf_op jit(solution)/shard_map/pallas_call | solution.py:363
  11.6 0.0 collective-permute-done.4.refs_5_
  11.6 0.0 collective-permute-done.5.refs_6_
  11.7 0.1 collective-permute-start.7
  11.8 0.5 %collective-permute-start.6 = (bf16[128,512]{1,0:T(8,128)(2,1)S(1)}, bf16[128,512]{1,0:T(8,128)(2,1)S(1)}, u32[]{:S(2)}, u32[]{:S(2)}) collective-permute-start(bf16[128,512]{1,0:T(8,128)(2,1)S(1)} %get-tuple-element.72), channel_id=1, source_target_pairs={{0,8},{8,0},{16,24},{24,16},{1,9},{9,1},{17,25},{25,17},{2,10},{10... | collective-permute-start | bytes 393224 | tf_op jit(solution)/shard_map/ppermute | solution.py:295
  12.3 0.1 collective-permute-start.2
  12.3 0.4 %collective-permute-start.8 = (bf16[256,512]{1,0:T(8,128)(2,1)S(1)}, bf16[256,512]{1,0:T(8,128)(2,1)S(1)}, u32[]{:S(2)}, u32[]{:S(2)}) collective-permute-start(bf16[256,512]{1,0:T(8,128)(2,1)S(1)} %bitcast.22), channel_id=1, source_target_pairs={{0,8},{8,0},{16,24},{24,16},{1,9},{9,1},{17,25},{25,17},{2,10},{10... | collective-permute-start | bytes 786440 | tf_op jit(solution)/shard_map/ppermute | solution.py:295
  12.8 0.7 %collective-permute-done.2.refs_3_ = s32[8,128]{1,0:T(8,128)S(1)} collective-permute-done((s32[8,128]{1,0:T(8,128)S(1)}, s32[8,128]{1,0:T(8,128)S(1)}, u32[]{:S(2)}, u32[]{:S(2)}) %collective-permute-start.2) | collective-permute-done | bytes 4128 | tf_op jit(solution)/shard_map/ppermute | solution.py:295
  13.4 0.0 collective-permute-done.7.refs_8_
  13.4 0.0 collective-permute-done.6.refs_7_
  13.5 2.6 %shard_map.164 = (bf16[384,512]{1,0:T(8,128)(2,1)S(1)}, bf16[4,384,640]{2,1,0:T(8,128)(2,1)S(1)}, bf16[256,512]{1,0:T(8,128)(2,1)S(1)}, bf16[128,512]{1,0:T(8,128)(2,1)}, f32[4,128]{1,0:T(4,128)S(1)}) custom-call(s32[8,128]{1,0:T(8,128)S(1)} %shard_map.162.info_ref.refs_0_, s32[8,128]{1,0:T(8,128)S(1)} %collective-permute-done.refs_1_, ...), custom_call_target="tpu_custom_call" | custom-call | flops 1000 | bytes 1000 | tf_op jit(solution)/shard_map/pallas_call | solution.py:391
  16.0 0.2 collective-permute-start.9
  16.2 1.5 %collective-permute-start.17 = (bf16[256,512]{1,0:T(8,128)(2,1)S(1)}, bf16[256,512]{1,0:T(8,128)(2,1)S(1)}, u32[]{:S(2)}, u32[]{:S(2)}) collective-permute-start(bf16[256,512]{1,0:T(8,128)(2,1)S(1)} %get-tuple-element.65.refs_4_), channel_id=1, source_target_pairs={{0,16},{8,24},{16,0},{24,8},{1,17},{9,25},{17,1},{25,9},{2,18},{10... | collective-permute-start | bytes 786440 | tf_op jit(solution)/shard_map/ppermute | solution.py:295
  17.8 0.0 collective-permute-done.8.refs_6_
  17.8 2.2 %shard_map.165 = (bf16[4,384,640]{2,1,0:T(8,128)(2,1)S(1)}, f32[24,128]{1,0:T(8,128)S(1)}) custom-call(s32[8,128]{1,0:T(8,128)S(1)} %shard_map.162.info_ref.refs_0_, s32[8,128]{1,0:T(8,128)S(1)} %collective-permute-done.refs_1_, s32[8,128]{1,0:T(8,128)S(1)} %collective-permute-done.1.refs_2_, s32[8,128]{1,0:T(8,128)S(1)} %collective-permute-done.2.refs_3_, ...), custom_call_target="tpu_custom_call" | custom-call | flops 1000 | bytes 1000 | tf_op jit(solution)/shard_map/pallas_call | solution.py:407
  19.9 1.5 %collective-permute-start.10 = (f32[24,128]{1,0:T(8,128)S(1)}, f32[24,128]{1,0:T(8,128)S(1)}, u32[]{:S(2)}, u32[]{:S(2)}) collective-permute-start(f32[24,128]{1,0:T(8,128)S(1)} %get-tuple-element.52), channel_id=1, source_target_pairs={{0,1},{1,0},{2,3},{3,2},{4,5},{5,4},{6,7},{7,6},{8,9},{9,8},{10,11... | collective-permute-start | bytes 36872 | tf_op jit(solution)/shard_map/ppermute | solution.py:302
  21.4 0.5 %shard_map.166.refs_4_ = bf16[256,512]{1,0:T(8,128)(2,1)S(1)} custom-call(bf16[4,384,640]{2,1,0:T(8,128)(2,1)S(1)} %get-tuple-element.54.ds_ref, bf16[4,640,128]{2,1,0:T(8,128)(2,1)S(1)} %get-tuple-element.43.refs_10_.qs_ref), custom_call_target="tpu_custom_call" | custom-call | flops 1000 | bytes 1000 | tf_op jit(solution)/shard_map/pallas_call | solution.py:419
  21.9 1.5 %collective-permute-start.11 = (bf16[256,512]{1,0:T(8,128)(2,1)S(1)}, bf16[256,512]{1,0:T(8,128)(2,1)S(1)}, u32[]{:S(2)}, u32[]{:S(2)}) collective-permute-start(bf16[256,512]{1,0:T(8,128)(2,1)S(1)} %shard_map.166.refs_4_), channel_id=1, source_target_pairs={{0,16},{8,24},{16,0},{24,8},{1,17},{9,25},{17,1},{25,9},{2,18},{10... | collective-permute-start | bytes 786440 | tf_op jit(solution)/shard_map/ppermute | solution.py:295
  23.4 0.2 collective-permute-done.10
  23.6 3.6 %collective-permute-start.14 = (f32[24,128]{1,0:T(8,128)S(1)}, f32[24,128]{1,0:T(8,128)S(1)}, u32[]{:S(2)}, u32[]{:S(2)}) collective-permute-start(f32[24,128]{1,0:T(8,128)S(1)} %add.15), channel_id=1, source_target_pairs={{0,6},{1,7},{2,4},{3,5},{4,2},{5,3},{6,0},{7,1},{8,14},{9,15},{10,... | collective-permute-start | bytes 36872 | tf_op jit(solution)/shard_map/ppermute | solution.py:302
  27.3 0.0 collective-permute-start.13
  27.3 0.8 %collective-permute-start.12 = (f32[24,128]{1,0:T(8,128)S(1)}, f32[24,128]{1,0:T(8,128)S(1)}, u32[]{:S(2)}, u32[]{:S(2)}) collective-permute-start(f32[24,128]{1,0:T(8,128)S(1)} %add.15), channel_id=1, source_target_pairs={{0,2},{1,3},{2,0},{3,1},{4,6},{5,7},{6,4},{7,5},{8,10},{9,11},{10,... | collective-permute-start | bytes 36872 | tf_op jit(solution)/shard_map/ppermute | solution.py:302
  28.0 1.7 %shard_map.167 = (bf16[128,2560]{1,0:T(8,128)(2,1)}, bf16[128,512]{1,0:T(8,128)(2,1)}) custom-call(bf16[4,384,640]{2,1,0:T(8,128)(2,1)S(1)} %get-tuple-element.54.ds_ref, bf16[384,512]{1,0:T(8,128)(2,1)S(1)} %get-tuple-element.49.refs_11_.ka_ref, bf16[4,640,128]{2,1,0:T(8,128)(2,1)S(1)} %get-tuple-element.43.refs_10_.qs_ref), custom_call_target="tpu_custom_call" | custom-call | flops 1000 | bytes 1000 | tf_op jit(solution)/shard_map/pallas_call | solution.py:432
  29.7 0.0 collective-permute-done.14
  29.7 2.1 %collective-permute-done.13 = f32[24,128]{1,0:T(8,128)S(1)} collective-permute-done((f32[24,128]{1,0:T(8,128)S(1)}, f32[24,128]{1,0:T(8,128)S(1)}, u32[]{:S(2)}, u32[]{:S(2)}) %collective-permute-start.13) | collective-permute-done | bytes 12320 | tf_op jit(solution)/shard_map/ppermute | solution.py:302
  31.8 0.0 collective-permute-done.12
  31.9 0.1 collective-permute-start.19
  31.9 0.5 %collective-permute-start.15 = (bf16[256,512]{1,0:T(8,128)(2,1)S(1)}, bf16[256,512]{1,0:T(8,128)(2,1)S(1)}, u32[]{:S(2)}, u32[]{:S(2)}) collective-permute-start(bf16[256,512]{1,0:T(8,128)(2,1)S(1)} %shard_map.166.refs_4_), channel_id=1, source_target_pairs={{0,8},{8,0},{16,24},{24,16},{1,9},{9,1},{17,25},{25,17},{2,10},{10... | collective-permute-start | bytes 786440 | tf_op jit(solution)/shard_map/ppermute | solution.py:295
  32.4 0.0 collective-permute-done.11.refs_5_
  32.4 0.1 collective-permute-start.16
  32.5 1.4 %collective-permute-start.20 = (f32[24,128]{1,0:T(8,128)S(1)}, f32[24,128]{1,0:T(8,128)S(1)}, u32[]{:S(2)}, u32[]{:S(2)}) collective-permute-start(f32[24,128]{1,0:T(8,128)S(1)} %add_add_fusion), channel_id=1, source_target_pairs={{0,16},{1,17},{2,18},{3,19},{4,20},{5,21},{6,22},{7,23},{8,24},{9,... | collective-permute-start | bytes 36872 | tf_op jit(solution)/shard_map/ppermute | solution.py:302
  34.0 0.0 collective-permute-done.18.refs_6_
  34.0 0.0 collective-permute-done.19.refs_7_
  34.0 0.9 %shard_map.169 = bf16[256,512]{1,0:T(8,128)(2,1)} custom-call(s32[8,128]{1,0:T(8,128)S(1)} %shard_map.162.info_ref.refs_0_, s32[8,128]{1,0:T(8,128)S(1)} %collective-permute-done.refs_1_, s32[8,128]{1,0:T(8,128)S(1)} %collective-permute-done.1.refs_2_, s32[8,128]{1,0:T(8,128)S(1)} %collective-permute-done.2.refs_3_, ...), custom_call_target="tpu_custom_call" | custom-call | flops 1000 | bytes 1000 | tf_op jit(solution)/shard_map/pallas_call | solution.py:343
  34.9 1.3 %collective-permute-done.20 = f32[24,128]{1,0:T(8,128)S(1)} collective-permute-done((f32[24,128]{1,0:T(8,128)S(1)}, f32[24,128]{1,0:T(8,128)S(1)}, u32[]{:S(2)}, u32[]{:S(2)}) %collective-permute-start.20) | collective-permute-done | bytes 12320 | tf_op jit(solution)/shard_map/ppermute | solution.py:302
  36.2 0.0 collective-permute-done.15.refs_6_
  36.2 0.9 %shard_map.168 = bf16[256,512]{1,0:T(8,128)(2,1)} custom-call(s32[8,128]{1,0:T(8,128)S(1)} %shard_map.162.info_ref.refs_0_, s32[8,128]{1,0:T(8,128)S(1)} %collective-permute-done.refs_1_, s32[8,128]{1,0:T(8,128)S(1)} %collective-permute-done.1.refs_2_, s32[8,128]{1,0:T(8,128)S(1)} %collective-permute-done.2.refs_3_, ...), custom_call_target="tpu_custom_call" | custom-call | flops 1000 | bytes 1000 | tf_op jit(solution)/shard_map/pallas_call | solution.py:343
  37.2 0.2 collective-permute-done.21.refs_1_
  37.4 0.6 %shard_map.170 = (f32[20,128]{1,0:T(8,128)}, f32[4,128]{1,0:T(4,128)}) custom-call(f32[24,128]{1,0:T(8,128)S(1)} %add.19.refs_0_, f32[24,128]{1,0:T(8,128)S(1)} %collective-permute-done.21.refs_1_), custom_call_target="tpu_custom_call" | custom-call | flops 1000 | bytes 1000 | tf_op jit(solution)/shard_map/pallas_call | solution.py:448
  (19 shorter events, 0.1 us)
Async XLA Ops:
  0.6 12.8 %copy-start.1 = (bf16[1,1,256,512]{3,2,1,0:T(8,128)(2,1)S(1)}, bf16[1,1,256,512]{3,2,1,0:T(8,128)(2,1)}, u32[]{:S(2)}) copy-start(bf16[1,1,256,512]{3,2,1,0:T(8,128)(2,1)} %param.14) | copy-start | bytes 786436
  0.6 11.7 %copy-start.2 = (bf16[1,1,256,512]{3,2,1,0:T(8,128)(2,1)S(1)}, bf16[1,1,256,512]{3,2,1,0:T(8,128)(2,1)}, u32[]{:S(2)}) copy-start(bf16[1,1,256,512]{3,2,1,0:T(8,128)(2,1)} %param.15) | copy-start | bytes 786436
  0.7 12.8 %copy-start = (bf16[1,1,128,512]{3,2,1,0:T(8,128)(2,1)S(1)}, bf16[1,1,128,512]{3,2,1,0:T(8,128)(2,1)}, u32[]{:S(2)}) copy-start(bf16[1,1,128,512]{3,2,1,0:T(8,128)(2,1)} %param.12) | copy-start | bytes 393220
  0.7 11.0 %collective-permute-start.4 = (bf16[256,512]{1,0:T(8,128)(2,1)}, bf16[256,512]{1,0:T(8,128)(2,1)S(1)}, u32[]{:S(2)}, u32[]{:S(2)}) collective-permute-start(bf16[256,512]{1,0:T(8,128)(2,1)} %bitcast.18), channel_id=1, source_target_pairs={{0,16},{8,24},{16,0},{24,8},{1,17},{9,25},{17,1},{25,9},{2,18},{10... | collective-permute-start | bytes 786440 | tf_op jit(solution)/shard_map/ppermute | solution.py:295
  3.7 8.0 %collective-permute-start.5 = (bf16[256,512]{1,0:T(8,128)(2,1)}, bf16[256,512]{1,0:T(8,128)(2,1)S(1)}, u32[]{:S(2)}, u32[]{:S(2)}) collective-permute-start(bf16[256,512]{1,0:T(8,128)(2,1)} %bitcast.19), channel_id=1, source_target_pairs={{0,8},{8,0},{16,24},{24,16},{1,9},{9,1},{17,25},{25,17},{2,10},{10... | collective-permute-start | bytes 786440 | tf_op jit(solution)/shard_map/ppermute | solution.py:295
  5.7 5.9 %collective-permute-start.1 = (s32[8,128]{1,0:T(8,128)S(1)}, s32[8,128]{1,0:T(8,128)S(1)}, u32[]{:S(2)}, u32[]{:S(2)}) collective-permute-start(s32[8,128]{1,0:T(8,128)S(1)} %shard_map.162.info_ref.refs_0_), channel_id=1, source_target_pairs={{0,8},{8,0},{16,24},{24,16},{1,9},{9,1},{17,25},{25,17},{2,10},{10... | collective-permute-start | bytes 12296 | tf_op jit(solution)/shard_map/ppermute | solution.py:295
  6.2 5.4 %collective-permute-start = (s32[8,128]{1,0:T(8,128)S(1)}, s32[8,128]{1,0:T(8,128)S(1)}, u32[]{:S(2)}, u32[]{:S(2)}) collective-permute-start(s32[8,128]{1,0:T(8,128)S(1)} %shard_map.162.info_ref.refs_0_), channel_id=1, source_target_pairs={{0,16},{8,24},{16,0},{24,8},{1,17},{9,25},{17,1},{25,9},{2,18},{10... | collective-permute-start | bytes 12296 | tf_op jit(solution)/shard_map/ppermute | solution.py:295
  6.3 9.7 %collective-permute-start.3 = (bf16[256,512]{1,0:T(8,128)(2,1)}, bf16[256,512]{1,0:T(8,128)(2,1)S(1)}, u32[]{:S(2)}, u32[]{:S(2)}) collective-permute-start(bf16[256,512]{1,0:T(8,128)(2,1)} %bitcast.21), channel_id=1, source_target_pairs={{0,16},{8,24},{16,0},{24,8},{1,17},{9,25},{17,1},{25,9},{2,18},{10... | collective-permute-start | bytes 786440 | tf_op jit(solution)/shard_map/ppermute | solution.py:295
  8.3 0.7 %copy-start.3 = (bf16[2560]{0:T(1024)(128)(2,1)S(1)}, bf16[2560]{0:T(1024)(128)(2,1)}, u32[]{:S(2)}) copy-start(bf16[2560]{0:T(1024)(128)(2,1)} %param.16) | copy-start | bytes 15364
  9.0 4.5 %copy-start.4 = (s32[1,1,2]{2,1,0:T(1,128)S(1)}, s32[1,1,2]{2,1,0:T(1,128)}, u32[]{:S(2)}) copy-start(s32[1,1,2]{2,1,0:T(1,128)} %param.21) | copy-start | bytes 28
  11.7 1.7 %collective-permute-start.7 = (bf16[128,512]{1,0:T(8,128)(2,1)S(1)}, bf16[128,512]{1,0:T(8,128)(2,1)S(1)}, u32[]{:S(2)}, u32[]{:S(2)}) collective-permute-start(bf16[128,512]{1,0:T(8,128)(2,1)S(1)} %get-tuple-element.71), channel_id=1, source_target_pairs={{0,8},{8,0},{16,24},{24,16},{1,9},{9,1},{17,25},{25,17},{2,10},{10... | collective-permute-start | bytes 393224 | tf_op jit(solution)/shard_map/ppermute | solution.py:295
  11.8 1.7 %collective-permute-start.6 = (bf16[128,512]{1,0:T(8,128)(2,1)S(1)}, bf16[128,512]{1,0:T(8,128)(2,1)S(1)}, u32[]{:S(2)}, u32[]{:S(2)}) collective-permute-start(bf16[128,512]{1,0:T(8,128)(2,1)S(1)} %get-tuple-element.72), channel_id=1, source_target_pairs={{0,8},{8,0},{16,24},{24,16},{1,9},{9,1},{17,25},{25,17},{2,10},{10... | collective-permute-start | bytes 393224 | tf_op jit(solution)/shard_map/ppermute | solution.py:295
  12.3 1.2 %collective-permute-start.2 = (s32[8,128]{1,0:T(8,128)S(1)}, s32[8,128]{1,0:T(8,128)S(1)}, u32[]{:S(2)}, u32[]{:S(2)}) collective-permute-start(s32[8,128]{1,0:T(8,128)S(1)} %collective-permute-done.refs_1_), channel_id=1, source_target_pairs={{0,8},{8,0},{16,24},{24,16},{1,9},{9,1},{17,25},{25,17},{2,10},{10... | collective-permute-start | bytes 12296 | tf_op jit(solution)/shard_map/ppermute | solution.py:295
  12.3 5.4 %collective-permute-start.8 = (bf16[256,512]{1,0:T(8,128)(2,1)S(1)}, bf16[256,512]{1,0:T(8,128)(2,1)S(1)}, u32[]{:S(2)}, u32[]{:S(2)}) collective-permute-start(bf16[256,512]{1,0:T(8,128)(2,1)S(1)} %bitcast.22), channel_id=1, source_target_pairs={{0,8},{8,0},{16,24},{24,16},{1,9},{9,1},{17,25},{25,17},{2,10},{10... | collective-permute-start | bytes 786440 | tf_op jit(solution)/shard_map/ppermute | solution.py:295
  16.0 1.7 %collective-permute-start.9 = (bf16[256,512]{1,0:T(8,128)(2,1)S(1)}, bf16[256,512]{1,0:T(8,128)(2,1)S(1)}, u32[]{:S(2)}, u32[]{:S(2)}) collective-permute-start(bf16[256,512]{1,0:T(8,128)(2,1)S(1)} %collective-permute-done.3.refs_5_), channel_id=1, source_target_pairs={{0,8},{8,0},{16,24},{24,16},{1,9},{9,1},{17,25},{25,17},{2,10},{10... | collective-permute-start | bytes 786440 | tf_op jit(solution)/shard_map/ppermute | solution.py:295
  16.2 15.6 %collective-permute-start.17 = (bf16[256,512]{1,0:T(8,128)(2,1)S(1)}, bf16[256,512]{1,0:T(8,128)(2,1)S(1)}, u32[]{:S(2)}, u32[]{:S(2)}) collective-permute-start(bf16[256,512]{1,0:T(8,128)(2,1)S(1)} %get-tuple-element.65.refs_4_), channel_id=1, source_target_pairs={{0,16},{8,24},{16,0},{24,8},{1,17},{9,25},{17,1},{25,9},{2,18},{10... | collective-permute-start | bytes 786440 | tf_op jit(solution)/shard_map/ppermute | solution.py:295
  19.9 3.7 %collective-permute-start.10 = (f32[24,128]{1,0:T(8,128)S(1)}, f32[24,128]{1,0:T(8,128)S(1)}, u32[]{:S(2)}, u32[]{:S(2)}) collective-permute-start(f32[24,128]{1,0:T(8,128)S(1)} %get-tuple-element.52), channel_id=1, source_target_pairs={{0,1},{1,0},{2,3},{3,2},{4,5},{5,4},{6,7},{7,6},{8,9},{9,8},{10,11... | collective-permute-start | bytes 36872 | tf_op jit(solution)/shard_map/ppermute | solution.py:302
  21.9 10.5 %collective-permute-start.11 = (bf16[256,512]{1,0:T(8,128)(2,1)S(1)}, bf16[256,512]{1,0:T(8,128)(2,1)S(1)}, u32[]{:S(2)}, u32[]{:S(2)}) collective-permute-start(bf16[256,512]{1,0:T(8,128)(2,1)S(1)} %shard_map.166.refs_4_), channel_id=1, source_target_pairs={{0,16},{8,24},{16,0},{24,8},{1,17},{9,25},{17,1},{25,9},{2,18},{10... | collective-permute-start | bytes 786440 | tf_op jit(solution)/shard_map/ppermute | solution.py:295
  23.6 6.1 %collective-permute-start.14 = (f32[24,128]{1,0:T(8,128)S(1)}, f32[24,128]{1,0:T(8,128)S(1)}, u32[]{:S(2)}, u32[]{:S(2)}) collective-permute-start(f32[24,128]{1,0:T(8,128)S(1)} %add.15), channel_id=1, source_target_pairs={{0,6},{1,7},{2,4},{3,5},{4,2},{5,3},{6,0},{7,1},{8,14},{9,15},{10,... | collective-permute-start | bytes 36872 | tf_op jit(solution)/shard_map/ppermute | solution.py:302
  27.3 4.6 %collective-permute-start.13 = (f32[24,128]{1,0:T(8,128)S(1)}, f32[24,128]{1,0:T(8,128)S(1)}, u32[]{:S(2)}, u32[]{:S(2)}) collective-permute-start(f32[24,128]{1,0:T(8,128)S(1)} %add.15), channel_id=1, source_target_pairs={{0,4},{1,5},{2,6},{3,7},{4,0},{5,1},{6,2},{7,3},{8,12},{9,13},{10,... | collective-permute-start | bytes 36872 | tf_op jit(solution)/shard_map/ppermute | solution.py:302
  27.3 4.6 %collective-permute-start.12 = (f32[24,128]{1,0:T(8,128)S(1)}, f32[24,128]{1,0:T(8,128)S(1)}, u32[]{:S(2)}, u32[]{:S(2)}) collective-permute-start(f32[24,128]{1,0:T(8,128)S(1)} %add.15), channel_id=1, source_target_pairs={{0,2},{1,3},{2,0},{3,1},{4,6},{5,7},{6,4},{7,5},{8,10},{9,11},{10,... | collective-permute-start | bytes 36872 | tf_op jit(solution)/shard_map/ppermute | solution.py:302
  29.7 4.2 %collective-permute-start.18 = (bf16[256,512]{1,0:T(8,128)(2,1)S(1)}, bf16[256,512]{1,0:T(8,128)(2,1)S(1)}, u32[]{:S(2)}, u32[]{:S(2)}) collective-permute-start(bf16[256,512]{1,0:T(8,128)(2,1)S(1)} %get-tuple-element.65.refs_4_), channel_id=1, source_target_pairs={{0,8},{8,0},{16,24},{24,16},{1,9},{9,1},{17,25},{25,17},{2,10},{10... | collective-permute-start | bytes 786440 | tf_op jit(solution)/shard_map/ppermute | solution.py:295
  31.9 2.1 %collective-permute-start.19 = (bf16[256,512]{1,0:T(8,128)(2,1)S(1)}, bf16[256,512]{1,0:T(8,128)(2,1)S(1)}, u32[]{:S(2)}, u32[]{:S(2)}) collective-permute-start(bf16[256,512]{1,0:T(8,128)(2,1)S(1)} %collective-permute-done.17.refs_5_), channel_id=1, source_target_pairs={{0,8},{8,0},{16,24},{24,16},{1,9},{9,1},{17,25},{25,17},{2,10},{10... | collective-permute-start | bytes 786440 | tf_op jit(solution)/shard_map/ppermute | solution.py:295
  31.9 4.3 %collective-permute-start.15 = (bf16[256,512]{1,0:T(8,128)(2,1)S(1)}, bf16[256,512]{1,0:T(8,128)(2,1)S(1)}, u32[]{:S(2)}, u32[]{:S(2)}) collective-permute-start(bf16[256,512]{1,0:T(8,128)(2,1)S(1)} %shard_map.166.refs_4_), channel_id=1, source_target_pairs={{0,8},{8,0},{16,24},{24,16},{1,9},{9,1},{17,25},{25,17},{2,10},{10... | collective-permute-start | bytes 786440 | tf_op jit(solution)/shard_map/ppermute | solution.py:295
  32.4 3.8 %collective-permute-start.16 = (bf16[256,512]{1,0:T(8,128)(2,1)S(1)}, bf16[256,512]{1,0:T(8,128)(2,1)S(1)}, u32[]{:S(2)}, u32[]{:S(2)}) collective-permute-start(bf16[256,512]{1,0:T(8,128)(2,1)S(1)} %collective-permute-done.11.refs_5_), channel_id=1, source_target_pairs={{0,8},{8,0},{16,24},{24,16},{1,9},{9,1},{17,25},{25,17},{2,10},{10... | collective-permute-start | bytes 786440 | tf_op jit(solution)/shard_map/ppermute | solution.py:295
  32.5 3.7 %collective-permute-start.20 = (f32[24,128]{1,0:T(8,128)S(1)}, f32[24,128]{1,0:T(8,128)S(1)}, u32[]{:S(2)}, u32[]{:S(2)}) collective-permute-start(f32[24,128]{1,0:T(8,128)S(1)} %add_add_fusion), channel_id=1, source_target_pairs={{0,16},{1,17},{2,18},{3,19},{4,20},{5,21},{6,22},{7,23},{8,24},{9,... | collective-permute-start | bytes 36872 | tf_op jit(solution)/shard_map/ppermute | solution.py:302
  36.2 1.2 %collective-permute-start.21 = (f32[24,128]{1,0:T(8,128)S(1)}, f32[24,128]{1,0:T(8,128)S(1)}, u32[]{:S(2)}, u32[]{:S(2)}) collective-permute-start(f32[24,128]{1,0:T(8,128)S(1)} %add.19.refs_0_), channel_id=1, source_target_pairs={{0,8},{8,0},{16,24},{24,16},{1,9},{9,1},{17,25},{25,17},{2,10},{10... | collective-permute-start | bytes 36872 | tf_op jit(solution)/shard_map/ppermute | solution.py:295

commit v4 on v3

--- a/solution.py
+++ b/solution.py
@@ -197,8 +197,9 @@
         high = sums.astype(jnp.bfloat16)
         low = (sums - high.astype(jnp.float32)).astype(jnp.bfloat16)
         keys = ka_ref[:, head(k)]
-        share = dot(high, keys, NN) + dot(low, keys, NN)
-        share_ref[k * gsize : (k + 1) * gsize, :] = share[:gsize, :] * score_scale
+        share = dot(jnp.concatenate([high, low], axis=0), keys, NN)
+        share = share[:gsize, :] + share[high.shape[0] : high.shape[0] + gsize, :]
+        share_ref[k * gsize : (k + 1) * gsize, :] = share * score_scale
 
     products(0)
     for k in range(kv_heads):

time: 38.2 us -> 38.2 us (level)
  no operation moved by 1% of the time
where the time goes in v4:
time: 38.2 us; the launch traced here: 38 us
  starting transfers between devices  17.9 us (47%)
  Pallas kernels  12.1 us (32%)
  waiting for transfers between devices  4.57 us (12%)
  between operations  2.73 us (7%)
  local copies, waits for them, and re-layouts  0.73 us (2%)
    ppermute x17, starting transfers between devices, shifted(): return lax.ppermute(x, axis, pairs)  10.5 us
    ppermute x5, starting transfers between devices, step_terms(): lax.ppermute(x, ('resp', 'dp'), [(i, i ^ flip) for i in range(count)])  7.33 us
    ppermute x5, waiting for transfers between devices, step_terms(): lax.ppermute(x, ('resp', 'dp'), [(i, i ^ flip) for i in range(count)])  3.63 us
    pallas_call x1, Pallas kernels, per_device(): call(functools.partial(self_kernel, kv_heads, gsize), [shape((kv_heads, g...  2.66 us
    pallas_call x1, Pallas kernels, per_device(): call(functools.partial(prob_kernel, kv_heads, gsize, count, len(keys_near...  2.57 us
    pallas_call x1, Pallas kernels, per_device(): call(functools.partial(score_kernel, kv_heads, gsize, count), [shape((kv_...  2.14 us
    pallas_call x2, Pallas kernels, summed(): call(functools.partial(sum_kernel, count), [shape((prefix_len, width_kv),...  1.83 us
    pallas_call x1, Pallas kernels, per_device(): call(functools.partial(grad_kernel, kv_heads, gsize), [shape((rows, width...  1.71 us
  transfers between devices with their start and end apart: 22, of which 5 were waited for; matrix products, arithmetic and copies ran while one was open for 0% of the time, Pallas kernels for 30%

profile of v4, /device:TPU:0, one launch (start us, length us, event | category | flops | bytes accessed | tf_op | source)
XLA Modules:
  0.0 38.0 jit_solution(5236460463915337126)
XLA Ops:
  0.6 0.0 copy-start.2
  0.7 0.0 copy-start
  0.7 3.0 %collective-permute-start.4 = (bf16[256,512]{1,0:T(8,128)(2,1)}, bf16[256,512]{1,0:T(8,128)(2,1)S(1)}, u32[]{:S(2)}, u32[]{:S(2)}) collective-permute-start(bf16[256,512]{1,0:T(8,128)(2,1)} %bitcast.18), channel_id=1, source_target_pairs={{0,16},{8,24},{16,0},{24,8},{1,17},{9,25},{17,1},{25,9},{2,18},{10... | collective-permute-start | bytes 786440 | tf_op jit(solution)/shard_map/ppermute | solution.py:296
  3.7 0.0 collective-permute-start.5
  5.6 0.1 shard_map.162.info_ref.refs_0_
  5.7 0.5 %collective-permute-start.1 = (s32[8,128]{1,0:T(8,128)S(1)}, s32[8,128]{1,0:T(8,128)S(1)}, u32[]{:S(2)}, u32[]{:S(2)}) collective-permute-start(s32[8,128]{1,0:T(8,128)S(1)} %shard_map.162.info_ref.refs_0_), channel_id=1, source_target_pairs={{0,8},{8,0},{16,24},{24,16},{1,9},{9,1},{17,25},{25,17},{2,10},{10... | collective-permute-start | bytes 12296 | tf_op jit(solution)/shard_map/ppermute | solution.py:296
  6.2 0.1 collective-permute-start
  6.3 1.9 %collective-permute-start.3 = (bf16[256,512]{1,0:T(8,128)(2,1)}, bf16[256,512]{1,0:T(8,128)(2,1)S(1)}, u32[]{:S(2)}, u32[]{:S(2)}) collective-permute-start(bf16[256,512]{1,0:T(8,128)(2,1)} %bitcast.21), channel_id=1, source_target_pairs={{0,16},{8,24},{16,0},{24,8},{1,17},{9,25},{17,1},{25,9},{2,18},{10... | collective-permute-start | bytes 786440 | tf_op jit(solution)/shard_map/ppermute | solution.py:296
  8.3 0.7 %copy-done.3 = bf16[2560]{0:T(1024)(128)(2,1)S(1)} copy-done((bf16[2560]{0:T(1024)(128)(2,1)S(1)}, bf16[2560]{0:T(1024)(128)(2,1)}, u32[]{:S(2)}) %copy-start.3) | copy-done | bytes 5144
  9.0 2.7 %shard_map.163 = (bf16[4,640,128]{2,1,0:T(8,128)(2,1)S(1)}, bf16[4,640,128]{2,1,0:T(8,128)(2,1)S(1)}, f32[4,128,640]{2,1,0:T(8,128)S(1)}, f32[4,128,640]{2,1,0:T(8,128)S(1)}) custom-call(s32[8,128]{1,0:T(8,128)S(1)} %shard_map.162.info_ref.refs_0_, bf16[20,128]{1,0:T(8,128)(2,1)S(1)} %bitcast.24, bf16[128,512]{1,0:T(8,128)(2,1)} %bitcast.16, ...), custom_call_target="tpu_custom_call" | custom-call | flops 1000 | bytes 1000 | tf_op jit(solution)/shard_map/pallas_call | solution.py:364
  11.6 0.0 collective-permute-done.1.refs_2_
  11.6 0.0 collective-permute-done.refs_1_
  11.6 0.0 collective-permute-done.4.refs_5_
  11.6 0.0 collective-permute-done.5.refs_6_
  11.7 0.1 collective-permute-start.7
  11.8 0.5 %collective-permute-start.6 = (bf16[128,512]{1,0:T(8,128)(2,1)S(1)}, bf16[128,512]{1,0:T(8,128)(2,1)S(1)}, u32[]{:S(2)}, u32[]{:S(2)}) collective-permute-start(bf16[128,512]{1,0:T(8,128)(2,1)S(1)} %get-tuple-element.72), channel_id=1, source_target_pairs={{0,8},{8,0},{16,24},{24,16},{1,9},{9,1},{17,25},{25,17},{2,10},{10... | collective-permute-start | bytes 393224 | tf_op jit(solution)/shard_map/ppermute | solution.py:296
  12.3 0.1 collective-permute-start.2
  12.3 0.4 %collective-permute-start.8 = (bf16[256,512]{1,0:T(8,128)(2,1)S(1)}, bf16[256,512]{1,0:T(8,128)(2,1)S(1)}, u32[]{:S(2)}, u32[]{:S(2)}) collective-permute-start(bf16[256,512]{1,0:T(8,128)(2,1)S(1)} %bitcast.22), channel_id=1, source_target_pairs={{0,8},{8,0},{16,24},{24,16},{1,9},{9,1},{17,25},{25,17},{2,10},{10... | collective-permute-start | bytes 786440 | tf_op jit(solution)/shard_map/ppermute | solution.py:296
  12.8 0.7 %collective-permute-done.2.refs_3_ = s32[8,128]{1,0:T(8,128)S(1)} collective-permute-done((s32[8,128]{1,0:T(8,128)S(1)}, s32[8,128]{1,0:T(8,128)S(1)}, u32[]{:S(2)}, u32[]{:S(2)}) %collective-permute-start.2) | collective-permute-done | bytes 4128 | tf_op jit(solution)/shard_map/ppermute | solution.py:296
  13.4 0.0 collective-permute-done.7.refs_8_
  13.4 0.0 collective-permute-done.6.refs_7_
  13.5 2.6 %shard_map.164 = (bf16[384,512]{1,0:T(8,128)(2,1)S(1)}, bf16[4,384,640]{2,1,0:T(8,128)(2,1)S(1)}, bf16[256,512]{1,0:T(8,128)(2,1)S(1)}, bf16[128,512]{1,0:T(8,128)(2,1)}, f32[4,128]{1,0:T(4,128)S(1)}) custom-call(s32[8,128]{1,0:T(8,128)S(1)} %shard_map.162.info_ref.refs_0_, s32[8,128]{1,0:T(8,128)S(1)} %collective-permute-done.refs_1_, ...), custom_call_target="tpu_custom_call" | custom-call | flops 1000 | bytes 1000 | tf_op jit(solution)/shard_map/pallas_call | solution.py:392
  16.0 0.0 collective-permute-done.3.refs_5_
  16.0 0.2 collective-permute-start.9
  16.2 1.5 %collective-permute-start.17 = (bf16[256,512]{1,0:T(8,128)(2,1)S(1)}, bf16[256,512]{1,0:T(8,128)(2,1)S(1)}, u32[]{:S(2)}, u32[]{:S(2)}) collective-permute-start(bf16[256,512]{1,0:T(8,128)(2,1)S(1)} %get-tuple-element.65.refs_4_), channel_id=1, source_target_pairs={{0,16},{8,24},{16,0},{24,8},{1,17},{9,25},{17,1},{25,9},{2,18},{10... | collective-permute-start | bytes 786440 | tf_op jit(solution)/shard_map/ppermute | solution.py:296
  17.8 2.1 %shard_map.165 = (bf16[4,384,640]{2,1,0:T(8,128)(2,1)S(1)}, f32[24,128]{1,0:T(8,128)S(1)}) custom-call(s32[8,128]{1,0:T(8,128)S(1)} %shard_map.162.info_ref.refs_0_, s32[8,128]{1,0:T(8,128)S(1)} %collective-permute-done.refs_1_, s32[8,128]{1,0:T(8,128)S(1)} %collective-permute-done.1.refs_2_, s32[8,128]{1,0:T(8,128)S(1)} %collective-permute-done.2.refs_3_, ...), custom_call_target="tpu_custom_call" | custom-call | flops 1000 | bytes 1000 | tf_op jit(solution)/shard_map/pallas_call | solution.py:408
  19.9 1.5 %collective-permute-start.10 = (f32[24,128]{1,0:T(8,128)S(1)}, f32[24,128]{1,0:T(8,128)S(1)}, u32[]{:S(2)}, u32[]{:S(2)}) collective-permute-start(f32[24,128]{1,0:T(8,128)S(1)} %get-tuple-element.52), channel_id=1, source_target_pairs={{0,1},{1,0},{2,3},{3,2},{4,5},{5,4},{6,7},{7,6},{8,9},{9,8},{10,11... | collective-permute-start | bytes 36872 | tf_op jit(solution)/shard_map/ppermute | solution.py:303
  21.4 0.5 %shard_map.166.refs_4_ = bf16[256,512]{1,0:T(8,128)(2,1)S(1)} custom-call(bf16[4,384,640]{2,1,0:T(8,128)(2,1)S(1)} %get-tuple-element.54.ds_ref, bf16[4,640,128]{2,1,0:T(8,128)(2,1)S(1)} %get-tuple-element.43.refs_10_.qs_ref), custom_call_target="tpu_custom_call" | custom-call | flops 1000 | bytes 1000 | tf_op jit(solution)/shard_map/pallas_call | solution.py:420
  21.9 1.5 %collective-permute-start.11 = (bf16[256,512]{1,0:T(8,128)(2,1)S(1)}, bf16[256,512]{1,0:T(8,128)(2,1)S(1)}, u32[]{:S(2)}, u32[]{:S(2)}) collective-permute-start(bf16[256,512]{1,0:T(8,128)(2,1)S(1)} %shard_map.166.refs_4_), channel_id=1, source_target_pairs={{0,16},{8,24},{16,0},{24,8},{1,17},{9,25},{17,1},{25,9},{2,18},{10... | collective-permute-start | bytes 786440 | tf_op jit(solution)/shard_map/ppermute | solution.py:296
  23.4 0.2 collective-permute-done.10
  23.6 3.6 %collective-permute-start.14 = (f32[24,128]{1,0:T(8,128)S(1)}, f32[24,128]{1,0:T(8,128)S(1)}, u32[]{:S(2)}, u32[]{:S(2)}) collective-permute-start(f32[24,128]{1,0:T(8,128)S(1)} %add.15), channel_id=1, source_target_pairs={{0,6},{1,7},{2,4},{3,5},{4,2},{5,3},{6,0},{7,1},{8,14},{9,15},{10,... | collective-permute-start | bytes 36872 | tf_op jit(solution)/shard_map/ppermute | solution.py:303
  27.2 0.0 collective-permute-start.13
  27.2 0.8 %collective-permute-start.12 = (f32[24,128]{1,0:T(8,128)S(1)}, f32[24,128]{1,0:T(8,128)S(1)}, u32[]{:S(2)}, u32[]{:S(2)}) collective-permute-start(f32[24,128]{1,0:T(8,128)S(1)} %add.15), channel_id=1, source_target_pairs={{0,2},{1,3},{2,0},{3,1},{4,6},{5,7},{6,4},{7,5},{8,10},{9,11},{10,... | collective-permute-start | bytes 36872 | tf_op jit(solution)/shard_map/ppermute | solution.py:303
  28.0 1.7 %shard_map.167 = (bf16[128,2560]{1,0:T(8,128)(2,1)}, bf16[128,512]{1,0:T(8,128)(2,1)}) custom-call(bf16[4,384,640]{2,1,0:T(8,128)(2,1)S(1)} %get-tuple-element.54.ds_ref, bf16[384,512]{1,0:T(8,128)(2,1)S(1)} %get-tuple-element.49.refs_11_.ka_ref, bf16[4,640,128]{2,1,0:T(8,128)(2,1)S(1)} %get-tuple-element.43.refs_10_.qs_ref), custom_call_target="tpu_custom_call" | custom-call | flops 1000 | bytes 1000 | tf_op jit(solution)/shard_map/pallas_call | solution.py:433
  29.7 0.0 collective-permute-start.18
  29.7 2.1 %collective-permute-done.13 = f32[24,128]{1,0:T(8,128)S(1)} collective-permute-done((f32[24,128]{1,0:T(8,128)S(1)}, f32[24,128]{1,0:T(8,128)S(1)}, u32[]{:S(2)}, u32[]{:S(2)}) %collective-permute-start.13) | collective-permute-done | bytes 12320 | tf_op jit(solution)/shard_map/ppermute | solution.py:303
  31.8 0.1 collective-permute-start.19
  31.9 0.5 %collective-permute-start.15 = (bf16[256,512]{1,0:T(8,128)(2,1)S(1)}, bf16[256,512]{1,0:T(8,128)(2,1)S(1)}, u32[]{:S(2)}, u32[]{:S(2)}) collective-permute-start(bf16[256,512]{1,0:T(8,128)(2,1)S(1)} %shard_map.166.refs_4_), channel_id=1, source_target_pairs={{0,8},{8,0},{16,24},{24,16},{1,9},{9,1},{17,25},{25,17},{2,10},{10... | collective-permute-start | bytes 786440 | tf_op jit(solution)/shard_map/ppermute | solution.py:296
  32.4 0.1 collective-permute-start.16
  32.5 1.4 %collective-permute-start.20 = (f32[24,128]{1,0:T(8,128)S(1)}, f32[24,128]{1,0:T(8,128)S(1)}, u32[]{:S(2)}, u32[]{:S(2)}) collective-permute-start(f32[24,128]{1,0:T(8,128)S(1)} %add_add_fusion), channel_id=1, source_target_pairs={{0,16},{1,17},{2,18},{3,19},{4,20},{5,21},{6,22},{7,23},{8,24},{9,... | collective-permute-start | bytes 36872 | tf_op jit(solution)/shard_map/ppermute | solution.py:303
  33.9 0.0 collective-permute-done.19.refs_7_
  33.9 0.9 %shard_map.169 = bf16[256,512]{1,0:T(8,128)(2,1)} custom-call(s32[8,128]{1,0:T(8,128)S(1)} %shard_map.162.info_ref.refs_0_, s32[8,128]{1,0:T(8,128)S(1)} %collective-permute-done.refs_1_, s32[8,128]{1,0:T(8,128)S(1)} %collective-permute-done.1.refs_2_, s32[8,128]{1,0:T(8,128)S(1)} %collective-permute-done.2.refs_3_, ...), custom_call_target="tpu_custom_call" | custom-call | flops 1000 | bytes 1000 | tf_op jit(solution)/shard_map/pallas_call | solution.py:344
  34.9 1.3 %collective-permute-done.20 = f32[24,128]{1,0:T(8,128)S(1)} collective-permute-done((f32[24,128]{1,0:T(8,128)S(1)}, f32[24,128]{1,0:T(8,128)S(1)}, u32[]{:S(2)}, u32[]{:S(2)}) %collective-permute-start.20) | collective-permute-done | bytes 12320 | tf_op jit(solution)/shard_map/ppermute | solution.py:303
  36.2 0.0 collective-permute-start.21
  36.2 0.0 collective-permute-done.15.refs_6_
  36.2 0.9 %shard_map.168 = bf16[256,512]{1,0:T(8,128)(2,1)} custom-call(s32[8,128]{1,0:T(8,128)S(1)} %shard_map.162.info_ref.refs_0_, s32[8,128]{1,0:T(8,128)S(1)} %collective-permute-done.refs_1_, s32[8,128]{1,0:T(8,128)S(1)} %collective-permute-done.1.refs_2_, s32[8,128]{1,0:T(8,128)S(1)} %collective-permute-done.2.refs_3_, ...), custom_call_target="tpu_custom_call" | custom-call | flops 1000 | bytes 1000 | tf_op jit(solution)/shard_map/pallas_call | solution.py:344
  37.1 0.2 collective-permute-done.21.refs_1_
  37.4 0.6 %shard_map.170 = (f32[20,128]{1,0:T(8,128)}, f32[4,128]{1,0:T(4,128)}) custom-call(f32[24,128]{1,0:T(8,128)S(1)} %add.19.refs_0_, f32[24,128]{1,0:T(8,128)S(1)} %collective-permute-done.21.refs_1_), custom_call_target="tpu_custom_call" | custom-call | flops 1000 | bytes 1000 | tf_op jit(solution)/shard_map/pallas_call | solution.py:449
  (19 shorter events, 0.1 us)
Async XLA Ops:
  0.6 12.8 %copy-start.1 = (bf16[1,1,256,512]{3,2,1,0:T(8,128)(2,1)S(1)}, bf16[1,1,256,512]{3,2,1,0:T(8,128)(2,1)}, u32[]{:S(2)}) copy-start(bf16[1,1,256,512]{3,2,1,0:T(8,128)(2,1)} %param.14) | copy-start | bytes 786436
  0.6 11.7 %copy-start.2 = (bf16[1,1,256,512]{3,2,1,0:T(8,128)(2,1)S(1)}, bf16[1,1,256,512]{3,2,1,0:T(8,128)(2,1)}, u32[]{:S(2)}) copy-start(bf16[1,1,256,512]{3,2,1,0:T(8,128)(2,1)} %param.15) | copy-start | bytes 786436
  0.7 12.8 %copy-start = (bf16[1,1,128,512]{3,2,1,0:T(8,128)(2,1)S(1)}, bf16[1,1,128,512]{3,2,1,0:T(8,128)(2,1)}, u32[]{:S(2)}) copy-start(bf16[1,1,128,512]{3,2,1,0:T(8,128)(2,1)} %param.12) | copy-start | bytes 393220
  0.7 11.0 %collective-permute-start.4 = (bf16[256,512]{1,0:T(8,128)(2,1)}, bf16[256,512]{1,0:T(8,128)(2,1)S(1)}, u32[]{:S(2)}, u32[]{:S(2)}) collective-permute-start(bf16[256,512]{1,0:T(8,128)(2,1)} %bitcast.18), channel_id=1, source_target_pairs={{0,16},{8,24},{16,0},{24,8},{1,17},{9,25},{17,1},{25,9},{2,18},{10... | collective-permute-start | bytes 786440 | tf_op jit(solution)/shard_map/ppermute | solution.py:296
  3.7 8.0 %collective-permute-start.5 = (bf16[256,512]{1,0:T(8,128)(2,1)}, bf16[256,512]{1,0:T(8,128)(2,1)S(1)}, u32[]{:S(2)}, u32[]{:S(2)}) collective-permute-start(bf16[256,512]{1,0:T(8,128)(2,1)} %bitcast.19), channel_id=1, source_target_pairs={{0,8},{8,0},{16,24},{24,16},{1,9},{9,1},{17,25},{25,17},{2,10},{10... | collective-permute-start | bytes 786440 | tf_op jit(solution)/shard_map/ppermute | solution.py:296
  5.7 5.9 %collective-permute-start.1 = (s32[8,128]{1,0:T(8,128)S(1)}, s32[8,128]{1,0:T(8,128)S(1)}, u32[]{:S(2)}, u32[]{:S(2)}) collective-permute-start(s32[8,128]{1,0:T(8,128)S(1)} %shard_map.162.info_ref.refs_0_), channel_id=1, source_target_pairs={{0,8},{8,0},{16,24},{24,16},{1,9},{9,1},{17,25},{25,17},{2,10},{10... | collective-permute-start | bytes 12296 | tf_op jit(solution)/shard_map/ppermute | solution.py:296
  6.2 5.4 %collective-permute-start = (s32[8,128]{1,0:T(8,128)S(1)}, s32[8,128]{1,0:T(8,128)S(1)}, u32[]{:S(2)}, u32[]{:S(2)}) collective-permute-start(s32[8,128]{1,0:T(8,128)S(1)} %shard_map.162.info_ref.refs_0_), channel_id=1, source_target_pairs={{0,16},{8,24},{16,0},{24,8},{1,17},{9,25},{17,1},{25,9},{2,18},{10... | collective-permute-start | bytes 12296 | tf_op jit(solution)/shard_map/ppermute | solution.py:296
  6.3 9.7 %collective-permute-start.3 = (bf16[256,512]{1,0:T(8,128)(2,1)}, bf16[256,512]{1,0:T(8,128)(2,1)S(1)}, u32[]{:S(2)}, u32[]{:S(2)}) collective-permute-start(bf16[256,512]{1,0:T(8,128)(2,1)} %bitcast.21), channel_id=1, source_target_pairs={{0,16},{8,24},{16,0},{24,8},{1,17},{9,25},{17,1},{25,9},{2,18},{10... | collective-permute-start | bytes 786440 | tf_op jit(solution)/shard_map/ppermute | solution.py:296
  8.3 0.7 %copy-start.3 = (bf16[2560]{0:T(1024)(128)(2,1)S(1)}, bf16[2560]{0:T(1024)(128)(2,1)}, u32[]{:S(2)}) copy-start(bf16[2560]{0:T(1024)(128)(2,1)} %param.16) | copy-start | bytes 15364
  9.0 4.5 %copy-start.4 = (s32[1,1,2]{2,1,0:T(1,128)S(1)}, s32[1,1,2]{2,1,0:T(1,128)}, u32[]{:S(2)}) copy-start(s32[1,1,2]{2,1,0:T(1,128)} %param.21) | copy-start | bytes 28
  11.7 1.7 %collective-permute-start.7 = (bf16[128,512]{1,0:T(8,128)(2,1)S(1)}, bf16[128,512]{1,0:T(8,128)(2,1)S(1)}, u32[]{:S(2)}, u32[]{:S(2)}) collective-permute-start(bf16[128,512]{1,0:T(8,128)(2,1)S(1)} %get-tuple-element.71), channel_id=1, source_target_pairs={{0,8},{8,0},{16,24},{24,16},{1,9},{9,1},{17,25},{25,17},{2,10},{10... | collective-permute-start | bytes 393224 | tf_op jit(solution)/shard_map/ppermute | solution.py:296
  11.8 1.7 %collective-permute-start.6 = (bf16[128,512]{1,0:T(8,128)(2,1)S(1)}, bf16[128,512]{1,0:T(8,128)(2,1)S(1)}, u32[]{:S(2)}, u32[]{:S(2)}) collective-permute-start(bf16[128,512]{1,0:T(8,128)(2,1)S(1)} %get-tuple-element.72), channel_id=1, source_target_pairs={{0,8},{8,0},{16,24},{24,16},{1,9},{9,1},{17,25},{25,17},{2,10},{10... | collective-permute-start | bytes 393224 | tf_op jit(solution)/shard_map/ppermute | solution.py:296
  12.3 1.2 %collective-permute-start.2 = (s32[8,128]{1,0:T(8,128)S(1)}, s32[8,128]{1,0:T(8,128)S(1)}, u32[]{:S(2)}, u32[]{:S(2)}) collective-permute-start(s32[8,128]{1,0:T(8,128)S(1)} %collective-permute-done.refs_1_), channel_id=1, source_target_pairs={{0,8},{8,0},{16,24},{24,16},{1,9},{9,1},{17,25},{25,17},{2,10},{10... | collective-permute-start | bytes 12296 | tf_op jit(solution)/shard_map/ppermute | solution.py:296
  12.3 5.4 %collective-permute-start.8 = (bf16[256,512]{1,0:T(8,128)(2,1)S(1)}, bf16[256,512]{1,0:T(8,128)(2,1)S(1)}, u32[]{:S(2)}, u32[]{:S(2)}) collective-permute-start(bf16[256,512]{1,0:T(8,128)(2,1)S(1)} %bitcast.22), channel_id=1, source_target_pairs={{0,8},{8,0},{16,24},{24,16},{1,9},{9,1},{17,25},{25,17},{2,10},{10... | collective-permute-start | bytes 786440 | tf_op jit(solution)/shard_map/ppermute | solution.py:296
  16.0 1.7 %collective-permute-start.9 = (bf16[256,512]{1,0:T(8,128)(2,1)S(1)}, bf16[256,512]{1,0:T(8,128)(2,1)S(1)}, u32[]{:S(2)}, u32[]{:S(2)}) collective-permute-start(bf16[256,512]{1,0:T(8,128)(2,1)S(1)} %collective-permute-done.3.refs_5_), channel_id=1, source_target_pairs={{0,8},{8,0},{16,24},{24,16},{1,9},{9,1},{17,25},{25,17},{2,10},{10... | collective-permute-start | bytes 786440 | tf_op jit(solution)/shard_map/ppermute | solution.py:296
  16.2 15.6 %collective-permute-start.17 = (bf16[256,512]{1,0:T(8,128)(2,1)S(1)}, bf16[256,512]{1,0:T(8,128)(2,1)S(1)}, u32[]{:S(2)}, u32[]{:S(2)}) collective-permute-start(bf16[256,512]{1,0:T(8,128)(2,1)S(1)} %get-tuple-element.65.refs_4_), channel_id=1, source_target_pairs={{0,16},{8,24},{16,0},{24,8},{1,17},{9,25},{17,1},{25,9},{2,18},{10... | collective-permute-start | bytes 786440 | tf_op jit(solution)/shard_map/ppermute | solution.py:296
  19.9 3.7 %collective-permute-start.10 = (f32[24,128]{1,0:T(8,128)S(1)}, f32[24,128]{1,0:T(8,128)S(1)}, u32[]{:S(2)}, u32[]{:S(2)}) collective-permute-start(f32[24,128]{1,0:T(8,128)S(1)} %get-tuple-element.52), channel_id=1, source_target_pairs={{0,1},{1,0},{2,3},{3,2},{4,5},{5,4},{6,7},{7,6},{8,9},{9,8},{10,11... | collective-permute-start | bytes 36872 | tf_op jit(solution)/shard_map/ppermute | solution.py:303
  21.9 10.5 %collective-permute-start.11 = (bf16[256,512]{1,0:T(8,128)(2,1)S(1)}, bf16[256,512]{1,0:T(8,128)(2,1)S(1)}, u32[]{:S(2)}, u32[]{:S(2)}) collective-permute-start(bf16[256,512]{1,0:T(8,128)(2,1)S(1)} %shard_map.166.refs_4_), channel_id=1, source_target_pairs={{0,16},{8,24},{16,0},{24,8},{1,17},{9,25},{17,1},{25,9},{2,18},{10... | collective-permute-start | bytes 786440 | tf_op jit(solution)/shard_map/ppermute | solution.py:296
  23.6 6.1 %collective-permute-start.14 = (f32[24,128]{1,0:T(8,128)S(1)}, f32[24,128]{1,0:T(8,128)S(1)}, u32[]{:S(2)}, u32[]{:S(2)}) collective-permute-start(f32[24,128]{1,0:T(8,128)S(1)} %add.15), channel_id=1, source_target_pairs={{0,6},{1,7},{2,4},{3,5},{4,2},{5,3},{6,0},{7,1},{8,14},{9,15},{10,... | collective-permute-start | bytes 36872 | tf_op jit(solution)/shard_map/ppermute | solution.py:303
  27.2 4.6 %collective-permute-start.13 = (f32[24,128]{1,0:T(8,128)S(1)}, f32[24,128]{1,0:T(8,128)S(1)}, u32[]{:S(2)}, u32[]{:S(2)}) collective-permute-start(f32[24,128]{1,0:T(8,128)S(1)} %add.15), channel_id=1, source_target_pairs={{0,4},{1,5},{2,6},{3,7},{4,0},{5,1},{6,2},{7,3},{8,12},{9,13},{10,... | collective-permute-start | bytes 36872 | tf_op jit(solution)/shard_map/ppermute | solution.py:303
  27.2 4.6 %collective-permute-start.12 = (f32[24,128]{1,0:T(8,128)S(1)}, f32[24,128]{1,0:T(8,128)S(1)}, u32[]{:S(2)}, u32[]{:S(2)}) collective-permute-start(f32[24,128]{1,0:T(8,128)S(1)} %add.15), channel_id=1, source_target_pairs={{0,2},{1,3},{2,0},{3,1},{4,6},{5,7},{6,4},{7,5},{8,10},{9,11},{10,... | collective-permute-start | bytes 36872 | tf_op jit(solution)/shard_map/ppermute | solution.py:303
  29.7 4.2 %collective-permute-start.18 = (bf16[256,512]{1,0:T(8,128)(2,1)S(1)}, bf16[256,512]{1,0:T(8,128)(2,1)S(1)}, u32[]{:S(2)}, u32[]{:S(2)}) collective-permute-start(bf16[256,512]{1,0:T(8,128)(2,1)S(1)} %get-tuple-element.65.refs_4_), channel_id=1, source_target_pairs={{0,8},{8,0},{16,24},{24,16},{1,9},{9,1},{17,25},{25,17},{2,10},{10... | collective-permute-start | bytes 786440 | tf_op jit(solution)/shard_map/ppermute | solution.py:296
  31.8 2.1 %collective-permute-start.19 = (bf16[256,512]{1,0:T(8,128)(2,1)S(1)}, bf16[256,512]{1,0:T(8,128)(2,1)S(1)}, u32[]{:S(2)}, u32[]{:S(2)}) collective-permute-start(bf16[256,512]{1,0:T(8,128)(2,1)S(1)} %collective-permute-done.17.refs_5_), channel_id=1, source_target_pairs={{0,8},{8,0},{16,24},{24,16},{1,9},{9,1},{17,25},{25,17},{2,10},{10... | collective-permute-start | bytes 786440 | tf_op jit(solution)/shard_map/ppermute | solution.py:296
  31.9 4.3 %collective-permute-start.15 = (bf16[256,512]{1,0:T(8,128)(2,1)S(1)}, bf16[256,512]{1,0:T(8,128)(2,1)S(1)}, u32[]{:S(2)}, u32[]{:S(2)}) collective-permute-start(bf16[256,512]{1,0:T(8,128)(2,1)S(1)} %shard_map.166.refs_4_), channel_id=1, source_target_pairs={{0,8},{8,0},{16,24},{24,16},{1,9},{9,1},{17,25},{25,17},{2,10},{10... | collective-permute-start | bytes 786440 | tf_op jit(solution)/shard_map/ppermute | solution.py:296
  32.4 3.8 %collective-permute-start.16 = (bf16[256,512]{1,0:T(8,128)(2,1)S(1)}, bf16[256,512]{1,0:T(8,128)(2,1)S(1)}, u32[]{:S(2)}, u32[]{:S(2)}) collective-permute-start(bf16[256,512]{1,0:T(8,128)(2,1)S(1)} %collective-permute-done.11.refs_5_), channel_id=1, source_target_pairs={{0,8},{8,0},{16,24},{24,16},{1,9},{9,1},{17,25},{25,17},{2,10},{10... | collective-permute-start | bytes 786440 | tf_op jit(solution)/shard_map/ppermute | solution.py:296
  32.5 3.7 %collective-permute-start.20 = (f32[24,128]{1,0:T(8,128)S(1)}, f32[24,128]{1,0:T(8,128)S(1)}, u32[]{:S(2)}, u32[]{:S(2)}) collective-permute-start(f32[24,128]{1,0:T(8,128)S(1)} %add_add_fusion), channel_id=1, source_target_pairs={{0,16},{1,17},{2,18},{3,19},{4,20},{5,21},{6,22},{7,23},{8,24},{9,... | collective-permute-start | bytes 36872 | tf_op jit(solution)/shard_map/ppermute | solution.py:303
  36.2 1.2 %collective-permute-start.21 = (f32[24,128]{1,0:T(8,128)S(1)}, f32[24,128]{1,0:T(8,128)S(1)}, u32[]{:S(2)}, u32[]{:S(2)}) collective-permute-start(f32[24,128]{1,0:T(8,128)S(1)} %add.19.refs_0_), channel_id=1, source_target_pairs={{0,8},{8,0},{16,24},{24,16},{1,9},{9,1},{17,25},{25,17},{2,10},{10... | collective-permute-start | bytes 36872 | tf_op jit(solution)/shard_map/ppermute | solution.py:296
